TPU v7x, 256 devices: a whole 4x4x8 slice. The times are simulated.
256 devices in a mesh: group: 16 (over z, x_hi), tp: 16 (over x_lo, y, core).
Axes of the slice: x: 4 (x_hi: 2, x_lo: 2; x = x_hi * 2 + x_lo), y: 4, z: 8, core: 2. Of those that a mesh axis runs over, the one named last changes fastest.
Arguments:
- hidden: bfloat16 [16, 16, 128, 8192], P('group', None, None, 'tp'), may hold values from -120 to 120
- norm_gain: bfloat16 [8192], P('tp'), may hold values from 0.099609375 to 1.8984375
- learner_weights: float32 [16, 8192, 2048], P('group', 'tp'), may hold values from -0.0625 to 0.0625
- plan: int32 [16, 16], P('group'), may hold values from 0 to 15, as said below
- block_fill: int32 [16, 16], P('group'), may hold values from 1 to 128
- block_pos: int32 [16, 16], P('group'), may hold values from 0 to 63
Outputs:
- kv_slots: bfloat16 [16, 32, 128, 2048], P('group', None, 'tp')
Inputs may be any that keep to these rules, and one draw needn't show every extreme that they name: `plan`: no group sends more than 2 blocks to one group; in every draw one group receives exactly 2 blocks from every group.
All inputs are finite; a program needn't handle non-finite values.
Results may differ from a plain program's by a relative error of at most 0.023.
Values may be sent and summed in bfloat16 or wider, within the bound.
No kernel may reach another device: no remote copies, remote signals or barrier semaphores. Data moves between devices by JAX's collectives and lax.ppermute only.
A program may use at most 128 MiB of HBM per device.

v0:
```python
import jax
import jax.numpy as jnp
from jax import lax
from jax.sharding import PartitionSpec as P

D = 8192
KV_HEADS = 8
HEAD = 128
BLOCK = 128
CAP = 2


def from_root(block, axis, holder):
    block = jnp.where(lax.axis_index(axis) == holder, block, jnp.zeros_like(block))
    return lax.psum(block, axis)


def rotate(key_value, positions):
    half_width = HEAD // 2
    freqs = 500000.0 ** (-(jnp.arange(half_width, dtype=jnp.float32) * 2.0) / HEAD)
    angles = positions.astype(jnp.float32)[..., None, None] * freqs
    cosine = jnp.cos(angles)
    sine = jnp.sin(angles)
    keys_part = key_value[..., : KV_HEADS * HEAD].reshape(positions.shape + (KV_HEADS, HEAD))
    first = keys_part[..., :half_width]
    second = keys_part[..., half_width:]
    turned = jnp.concatenate([first * cosine - second * sine, second * cosine + first * sine], -1)
    turned = turned.reshape(positions.shape + (KV_HEADS * HEAD,))
    return jnp.concatenate([turned, key_value[..., KV_HEADS * HEAD :]], -1)


def body(hidden, norm_gain, learner_weights, plan, block_fill, block_pos):
    groups = lax.axis_size("group")
    parts = lax.axis_size("tp")
    slots_total = groups * CAP
    tok_share = BLOCK // parts
    blocks_held = hidden.shape[1]
    weights = from_root(learner_weights[0].astype(jnp.bfloat16), "group", 0)
    targets = plan[0]
    one_hot = (targets[:, None] == jnp.arange(groups, dtype=jnp.int32)[None, :]).astype(jnp.int32)
    earlier = jnp.cumsum(one_hot, 0) - one_hot
    slot_index = jnp.sum(earlier * one_hot, -1)
    target_slot = targets * CAP + slot_index
    matches = target_slot[None, :] == jnp.arange(slots_total, dtype=jnp.int32)[:, None]
    filled = jnp.any(matches, 1)
    source_block = jnp.sum(
        matches.astype(jnp.int32) * jnp.arange(blocks_held, dtype=jnp.int32)[None, :], 1
    )
    outgoing = jnp.take(hidden[0], source_block, axis=0) * filled[:, None, None].astype(
        jnp.bfloat16
    )
    outgoing = outgoing.reshape(groups, CAP, BLOCK, hidden.shape[3])
    send_fill = jnp.where(filled, jnp.take(block_fill[0], source_block), 0).reshape(groups, CAP)
    send_pos = jnp.where(filled, jnp.take(block_pos[0], source_block), 0).reshape(groups, CAP)
    incoming, got_fill, got_pos = (
        lax.all_to_all(outgoing, "group", split_axis=0, concat_axis=0, tiled=True),
        lax.all_to_all(send_fill, "group", split_axis=0, concat_axis=0, tiled=True),
        lax.all_to_all(send_pos, "group", split_axis=0, concat_axis=0, tiled=True),
    )
    incoming = incoming.reshape(slots_total, BLOCK, hidden.shape[3])
    values = incoming.astype(jnp.float32)
    squares = lax.psum(jnp.sum(values * values, -1), "tp")
    inverse = lax.rsqrt(squares / D + 1e-05)
    normed = (values * inverse[..., None] * norm_gain.astype(jnp.float32)).astype(jnp.bfloat16)
    key_value = lax.psum_scatter(
        jnp.einsum("ncd,dk->cnk", normed, weights, preferred_element_type=jnp.float32).astype(
            jnp.bfloat16
        ),
        "tp",
        scatter_dimension=0,
        tiled=True,
    ).astype(jnp.float32)
    token_index = lax.axis_index("tp") * tok_share + jnp.arange(tok_share, dtype=jnp.int32)
    positions = got_pos.reshape(slots_total)[None, :] * BLOCK + token_index[:, None]
    rotated = rotate(key_value, positions)
    live_mask = token_index[:, None] < got_fill.reshape(slots_total)[None, :]
    finished = jnp.where(live_mask[..., None], rotated, 0.0).astype(jnp.bfloat16)
    result = jnp.transpose(finished, (1, 0, 2))
    return result[None]


def solution(mesh):
    in_specs = (
        P("group", None, None, "tp"),
        P("tp"),
        P("group", "tp", None),
        P("group", None),
        P("group", None),
        P("group", None),
    )
    out_specs = P("group", None, "tp", None)
    return jax.shard_map(body, mesh=mesh, in_specs=in_specs, out_specs=out_specs, check_vma=False)
```

profile of v0, /device:TPU:8, one launch (start us, length us, event | category | flops | bytes accessed | tf_op | source)
XLA Modules:
  0.0 401.3 jit_solution(14549404424021253084)
XLA Ops:
  6.5 0.9 fusion.6
  7.4 0.8 select_reduce_fusion.1
  8.3 0.7 fusion.8
  9.4 2.7 gather_fusion
  12.1 4.6 %select_multiply_fusion = bf16[16,2,128,512]{3,2,1,0:T(8,128)(2,1)} fusion(bf16[16,2,128,512]{3,2,1,0:T(8,128)(2,1)} %bitcast.45, pred[16,2]{1,0:T(8,128)(4,1)S(1)} %compare_and_fusion, bf16[16,2]{1,0:T(8,128)(2,1)S(1)} %reshape.153), kind=kLoop, calls=%fused_computation.8 | loop fusion | flops 4194304 | bytes 8388704 | tf_op jit(solution)/shard_map/mul | solution.py:49
  16.7 11.1 %all-to-all-start.1 = ((bf16[16,2,128,512]{3,2,1,0:T(8,128)(2,1)}), bf16[16,2,128,512]{3,2,1,0:T(8,128)(2,1)}, u32[]{:S(2)}, u32[]{:S(2)}) async-start(bf16[16,2,128,512]{3,2,1,0:T(8,128)(2,1)} %select_multiply_fusion), calls=%async_computation.1 | async-start | bytes 8388608 | tf_op jit(solution)/shard_map/all_to_all | solution.py:56
  27.9 3.4 copy.17
  31.2 1.4 select_bitcast_fusion
  32.8 99.9 %all-to-all-done.1 = bf16[16,2,128,512]{3,2,1,0:T(8,128)(2,1)} async-done(((bf16[16,2,128,512]{3,2,1,0:T(8,128)(2,1)}), bf16[16,2,128,512]{3,2,1,0:T(8,128)(2,1)}, u32[]{:S(2)}, u32[]{:S(2)}) %all-to-all-start.1) | async-done | bytes 4194336 | tf_op jit(solution)/shard_map/all_to_all | solution.py:56
  132.6 3.1 multiply_reduce_fusion
  135.8 50.1 %psum.15 = f32[32,128]{1,0:T(8,128)S(1)} all-reduce(f32[32,128]{1,0:T(8,128)S(1)} %bitcast.48), channel_id=1, replica_groups=mesh['group'=16,'tp'=16] {'tp'}, use_global_device_ids=true, to_apply=%region_6.8 | all-reduce | flops 4096 | bytes 32768 | tf_op jit(solution)/shard_map/psum | solution.py:62
  185.9 4.1 %fusion.1 = bf16[32,128,512]{2,1,0:T(8,128)(2,1)} fusion(f32[512]{0:T(512)S(1)} %convert_element_type.60, f32[32,128]{1,0:T(8,128)S(1)} %add_rsqrt_fusion, bf16[16,2,128,512]{3,2,1,0:T(8,128)(2,1)} %all-to-all-done.1), kind=kLoop, calls=%fused_computation.6 | loop fusion | flops 8388608 | bytes 8407040 | tf_op jit(solution)/shard_map/convert_element_type | solution.py:64
  190.0 65.3 %all-reduce.2.cloned.1.call-done = bf16[512,2048]{0,1:T(8,128)(2,1)} async-done(((bf16[512,2048]{0,1:T(8,128)(2,1)}), bf16[512,2048]{0,1:T(8,128)(2,1)}) %all-reduce.2.cloned.1.call-update) | async-done | bytes 2097168 | tf_op jit(solution)/shard_map/psum | solution.py:15
  255.3 14.2 %convert_bitcast_fusion = bf16[128,32,2048]{0,2,1:T(8,128)(2,1)} fusion(bf16[32,128,512]{2,1,0:T(8,128)(2,1)} %fusion.1, bf16[512,2048]{0,1:T(8,128)(2,1)} %all-reduce.2.cloned.1.call-done), kind=kOutput, calls=%fused_computation.3 | convolution fusion | flops 8598323200 | bytes 23068672 | tf_op jit(solution)/shard_map/ncd,dk->cnk/dot_general | solution.py:66
  269.5 24.0 %copy.18 = bf16[128,32,2048]{2,1,0:T(8,128)(2,1)} copy(bf16[128,32,2048]{0,2,1:T(8,128)(2,1)} %convert_bitcast_fusion) | data formatting | bytes 33554432 | tf_op jit(solution)/shard_map/convert_element_type | solution.py:66
  293.6 0.6 copy-done.2
  294.2 0.7 gather_fusion.1
  294.9 0.7 gather_fusion.2
  295.6 0.7 all_to_all.18
  296.3 5.4 %all-to-all-start.2 = ((s32[16,1,2]{2,1,0:T(1,128)}), s32[16,1,2]{2,1,0:T(1,128)S(1)}, u32[]{:S(2)}, u32[]{:S(2)}) async-start(s32[16,1,2]{2,1,0:T(1,128)} %bitcast.15), calls=%async_computation.3 | async-start | bytes 16384 | tf_op jit(solution)/shard_map/all_to_all | solution.py:58
  301.8 0.7 all_to_all.15
  302.5 9.2 %all-to-all-done.2 = s32[16,1,2]{2,1,0:T(1,128)S(1)} async-done(((s32[16,1,2]{2,1,0:T(1,128)}), s32[16,1,2]{2,1,0:T(1,128)S(1)}, u32[]{:S(2)}, u32[]{:S(2)}) %all-to-all-start.2) | async-done | bytes 160 | tf_op jit(solution)/shard_map/all_to_all | solution.py:58
  311.7 3.4 all-to-all-start
  315.2 9.8 %all-to-all-done = s32[16,1,2]{2,1,0:T(1,128)S(1)} async-done(((s32[16,1,2]{2,1,0:T(1,128)}), s32[16,1,2]{2,1,0:T(1,128)S(1)}, u32[]{:S(2)}, u32[]{:S(2)}) %all-to-all-start) | async-done | bytes 160 | tf_op jit(solution)/shard_map/all_to_all | solution.py:57
  325.6 0.7 reduce.8
  326.5 0.5 multiply_cosine_fusion
  327.0 61.3 %reduce-scatter.2.cloned.1.call-done = bf16[8,32,2048]{2,1,0:T(8,128)(2,1)} async-done(((bf16[128,32,2048]{2,1,0:T(8,128)(2,1)}), bf16[8,32,2048]{2,1,0:T(8,128)(2,1)}) %reduce-scatter.2.cloned.1.call-update) | async-done | bytes 1048592 | tf_op jit(solution)/shard_map/reduce_scatter | solution.py:65
  388.4 1.1 slice.22
  389.7 0.5 multiply_subtract_fusion
  390.6 1.0 reshape.152
  391.6 1.3 fusion.4
  392.9 1.5 copy.20
  (39 shorter events, 1.9 us)
Async XLA Ops:
  6.5 2.8 copy-start
  16.7 115.9 %all-to-all-start.1 = ((bf16[16,2,128,512]{3,2,1,0:T(8,128)(2,1)}), bf16[16,2,128,512]{3,2,1,0:T(8,128)(2,1)}, u32[]{:S(2)}, u32[]{:S(2)}) async-start(bf16[16,2,128,512]{3,2,1,0:T(8,128)(2,1)} %select_multiply_fusion), calls=%async_computation.1 | async-start | bytes 8388608 | tf_op jit(solution)/shard_map/all_to_all | solution.py:56
  27.8 227.5 %all-reduce.2.cloned.1.call-start = ((), (), s32[]{:S(2)}) async-start(), calls=%async_computation.4 | async-start | bytes 4194304 | tf_op jit(solution)/shard_map/psum | solution.py:15
  31.2 1.5 copy-start.4
  32.7 355.7 %reduce-scatter.2.cloned.1.call-start = ((), (), s32[]{:S(2)}) async-start(), calls=%async_computation.5 | async-start | bytes 17825792 | tf_op jit(solution)/shard_map/reduce_scatter | solution.py:65
  293.5 0.7 copy-start.2
  293.6 1.4 copy-start.3
  296.3 15.4 %all-to-all-start.2 = ((s32[16,1,2]{2,1,0:T(1,128)}), s32[16,1,2]{2,1,0:T(1,128)S(1)}, u32[]{:S(2)}, u32[]{:S(2)}) async-start(s32[16,1,2]{2,1,0:T(1,128)} %bitcast.15), calls=%async_computation.3 | async-start | bytes 16384 | tf_op jit(solution)/shard_map/all_to_all | solution.py:58
  311.7 13.4 %all-to-all-start = ((s32[16,1,2]{2,1,0:T(1,128)}), s32[16,1,2]{2,1,0:T(1,128)S(1)}, u32[]{:S(2)}, u32[]{:S(2)}) async-start(s32[16,1,2]{2,1,0:T(1,128)} %bitcast.4), calls=%async_computation | async-start | bytes 16384 | tf_op jit(solution)/shard_map/all_to_all | solution.py:57
  389.5 2.1 slice-start
  389.7 4.7 %copy-start.1 = (bf16[1,16,128,512]{3,2,1,0:T(8,128)(2,1)S(1)}, bf16[1,16,128,512]{3,2,1,0:T(8,128)(2,1)}, u32[]{:S(2)}) copy-start(bf16[1,16,128,512]{3,2,1,0:T(8,128)(2,1)} %param.8) | copy-start | bytes 6291460
Sparse Core Ops, SparseCore 0:
  32.8 222.4 all-reduce.1
  293.7 94.6 reduce-scatter.1
where the time goes:
time: 406 us; the launch traced here: 401 us
  waiting for transfers between devices  246 us (61%)
  blocking collectives  50.1 us (12%)
  local copies, waits for them, and re-layouts  38.3 us (9%)
  starting transfers between devices  20 us (5%)
  other arithmetic  19.4 us (5%)
  matrix products  14.2 us (3%)
  between operations  13.6 us (3%)
    all_to_all x1, waiting for transfers between devices, body(): lax.all_to_all(outgoing, 'group', split_axis=0, concat_axis=0, tiled=True)  99.9 us
    psum x1, waiting for transfers between devices, from_root(): return lax.psum(block, axis)  65.3 us
    reduce_scatter x1, waiting for transfers between devices, body(): lax.psum_scatter(jnp.einsum('ncd,dk->cnk', normed, weights, preferred_ele...  61.3 us
    psum x1, blocking collectives, body(): squares = lax.psum(jnp.sum(values * values, -1), 'tp')  50.1 us
    convert_element_type x1, local copies, waits for them, and re-layouts, body(): jnp.einsum('ncd,dk->cnk', normed, weights, preferred_element_type=jnp.flo...  24 us
    dot_general x1, matrix products, body(): jnp.einsum('ncd,dk->cnk', normed, weights, preferred_element_type=jnp.flo...  14.2 us
    all_to_all x1, starting transfers between devices, body(): lax.all_to_all(outgoing, 'group', split_axis=0, concat_axis=0, tiled=True)  11.1 us
    all_to_all x1, waiting for transfers between devices, body(): lax.all_to_all(send_fill, 'group', split_axis=0, concat_axis=0, tiled=True)  9.81 us
  transfers between devices with their start and end apart: 5, of which 5 were waited for; matrix products, arithmetic and copies ran while one was open for 4% of the time, Pallas kernels for 0%

commit v1 on v0

v1 whole, which is shorter than its diff:
```python
import functools

import jax
import jax.numpy as jnp
from jax import lax
from jax.experimental import pallas as pl
from jax.experimental.pallas import tpu as pltpu
from jax.sharding import PartitionSpec as P

D = 8192
KV_HEADS = 8
HEAD = 128
BLOCK = 128
CAP = 2
KVW = 2048
Z = 8
X = 2
Y = 4
PIECES = 8
PIECE = KVW // PIECES
CHUNKS = ((0, 1, 2, 3, 4), (5, 6, 7))
BF16 = jnp.bfloat16
F32 = jnp.float32


def tp_pairs(dx, dy, dc):
    pairs = []
    for t in range(16):
        x, y, c = t // 8, (t // 2) % 4, t % 2
        pairs.append((t, ((x ^ dx) * 4 + (y + dy) % Y) * 2 + (c ^ dc)))
    return pairs


def ring_pairs():
    pairs = []
    for g in range(16):
        for t in range(16):
            z, h, c = g // 2, g % 2, t % 2
            there = (z + (1 if c == 0 else -1)) % Z
            pairs.append((g * 16 + t, (there * 2 + h) * 16 + t))
    return pairs


def to_core(value):
    return lax.ppermute(value, "tp", tp_pairs(0, 0, 1))


def product_kernel(count, rows_ref, *refs):
    pieces, outs = refs[:count], refs[count:]
    for dy in range(Y):
        for k in range(count):
            outs[dy][:, k * PIECE : (k + 1) * PIECE] = jnp.dot(
                rows_ref[dy], pieces[k][...], preferred_element_type=F32
            ).astype(BF16)


def product(rows, pieces):
    count = len(pieces)
    half = rows.shape[1]
    width = count * PIECE
    vmem = pl.BlockSpec(memory_space=pltpu.VMEM)
    return pl.pallas_call(
        functools.partial(product_kernel, count),
        out_shape=[jax.ShapeDtypeStruct((half, width), BF16)] * Y,
        in_specs=[vmem] * (1 + count),
        out_specs=[vmem] * Y,
        compiler_params=pltpu.CompilerParams(vmem_limit_bytes=40 * 2**20),
        cost_estimate=pl.CostEstimate(
            flops=2 * Y * half * width * rows.shape[2],
            bytes_accessed=2 * (rows.size + width * rows.shape[2] + Y * half * width),
            transcendentals=0,
        ),
    )(rows, *pieces)


def finish_kernel(where_ref, source_ref, filled_ref, cos_ref, sin_ref, scale_ref, *refs):
    out_ref, done = refs[-2:]
    scale = scale_ref[...]
    at = 0
    for chunk in CHUNKS:
        parts, at = refs[at : at + Y + 1], at + Y + 1
        for n, k in enumerate(chunk):
            column = where_ref[k]
            is_key = jnp.where(column < PIECES // 2, 1.0, 0.0).astype(F32)
            for head in range(PIECE // HEAD):
                cols = slice(n * PIECE + head * HEAD, n * PIECE + (head + 1) * HEAD)
                value = parts[0][:, cols].astype(F32)
                for part in parts[1:]:
                    value = value + part[:, cols].astype(F32)
                other = pltpu.roll(value, HEAD // 2, 1)
                turned = value * cos_ref[...] + other * sin_ref[...]
                value = jnp.where(is_key > 0.5, turned, value) * scale
                start = pl.multiple_of(column * PIECE + head * HEAD, HEAD)
                done[:, pl.ds(start, HEAD)] = value
    tok = 8
    for group in range(out_ref.shape[0]):
        both = []
        for slot in range(CAP):
            j = group * CAP + slot
            first = pl.multiple_of(source_ref[j] * tok, tok)
            keep = filled_ref[j] > 0
            both.append(jnp.where(keep, done[pl.ds(first, tok), :], 0.0))
        out_ref[group] = jnp.concatenate(both, 0).astype(BF16)


def finish(column_of, source, filled, cosine, sine, scale, chunks, groups):
    rows = cosine.shape[0]
    smem = pl.BlockSpec(memory_space=pltpu.SMEM)
    vmem = pl.BlockSpec(memory_space=pltpu.VMEM)
    flat, specs = [], []
    for chunk in chunks:
        for part in chunk:
            flat.append(part)
            specs.append(pl.BlockSpec((rows, part.shape[1]), lambda i: (0, 0)))
    return pl.pallas_call(
        finish_kernel,
        grid=(1,),
        out_shape=jax.ShapeDtypeStruct((groups, CAP * 8, KVW), BF16),
        in_specs=[smem] * 3 + [vmem] * 3 + specs,
        out_specs=vmem,
        scratch_shapes=[pltpu.VMEM((rows, KVW), F32)],
        compiler_params=pltpu.CompilerParams(vmem_limit_bytes=40 * 2**20),
    )(column_of, source, filled, cosine, sine, scale, *flat)


def spread_weights(weights, group, core):
    z = group // 2
    pieces = [weights[:, k * PIECE : (k + 1) * PIECE] for k in range(PIECES)]
    own = jnp.where(group == 0, pieces[0], jnp.zeros_like(pieces[0]))
    for k in range(1, PIECES):
        own = own + lax.ppermute(pieces[k], "group", [(0, 2 * k)])
    own = own + lax.ppermute(own, "group", [(2 * k, 2 * k + 1) for k in range(Z)])
    partner = to_core(own)
    first = core == 0
    own = jnp.concatenate([jnp.where(first, own, partner), jnp.where(first, partner, own)], 0)
    held = [own]
    moving = own
    for step in range(1, Z // 2):
        moving = lax.ppermute(moving, ("group", "tp"), ring_pairs())
        held += [moving, to_core(moving)]
    features = weights.shape[0]
    half = lax.dynamic_slice_in_dim(moving, core * features, features, 0)
    half = lax.ppermute(half, ("group", "tp"), ring_pairs())
    partner = to_core(half)
    held.append(
        jnp.concatenate([jnp.where(first, half, partner), jnp.where(first, partner, half)], 0)
    )
    sign = jnp.where(first, -1, 1)
    steps = [0]
    for step in range(1, Z // 2):
        steps += [step, -step]
    steps.append(Z // 2)
    column_of = (z + sign * jnp.array(steps, jnp.int32) + Z) % Z
    return held, column_of.astype(jnp.int32)


def body(hidden, norm_gain, learner_weights, plan, block_fill, block_pos):
    groups = lax.axis_size("group")
    slots_total = groups * CAP
    blocks = hidden.shape[1]
    features = hidden.shape[3]
    group = lax.axis_index("group")
    tp = lax.axis_index("tp")
    x, y, core = tp // 8, (tp // 2) % Y, tp % 2
    tok = BLOCK // 16
    rows = blocks * tok

    weights = learner_weights[0].astype(BF16).astype(F32) * norm_gain.astype(F32)[:, None]
    held, column_of = spread_weights(weights.astype(BF16), group, core)

    by_owner = hidden[0].reshape(blocks, 16, tok, features).transpose(1, 0, 2, 3)
    dy = jnp.arange(Y, dtype=jnp.int32)[:, None]
    dx = jnp.arange(X, dtype=jnp.int32)[None, :]
    owner = ((x ^ dx) * Y + (y + dy) % Y).reshape(-1) * 2
    mine = jnp.take(by_owner, owner + core, axis=0)
    theirs = to_core(jnp.take(by_owner, owner + 1 - core, axis=0))
    first = core == 0
    rows_all = jnp.concatenate(
        [jnp.where(first, mine, theirs), jnp.where(first, theirs, mine)], -1
    ).reshape(Y, X * rows, 2 * features)

    squares = jnp.sum(jnp.square(rows_all.astype(F32)), -1).reshape(Y, X, rows)
    total = squares[0]
    for step in range(1, Y):
        total = total + lax.ppermute(squares[step], "tp", tp_pairs(0, step, 0))
    total = total[0] + lax.ppermute(total[1], "tp", tp_pairs(1, 0, 0))
    inverse = lax.rsqrt(total / D + 1e-05)

    token = tp * tok + jnp.arange(tok, dtype=jnp.int32)
    positions = (block_pos[0][:, None] * BLOCK + token[None, :]).reshape(rows)
    live = (token[None, :] < block_fill[0][:, None]).reshape(rows)
    half_width = HEAD // 2
    freqs = 500000.0 ** (-(jnp.arange(half_width, dtype=F32) * 2.0) / HEAD)
    angles = positions.astype(F32)[:, None] * freqs
    cosine, sine = jnp.cos(angles), jnp.sin(angles)
    cosine = jnp.concatenate([cosine, cosine], -1)
    sine = jnp.concatenate([-sine, sine], -1)
    scale = jnp.where(live, inverse, 0.0)[:, None]

    targets = plan[0]
    one_hot = (targets[:, None] == jnp.arange(groups, dtype=jnp.int32)[None, :]).astype(jnp.int32)
    earlier = jnp.cumsum(one_hot, 0) - one_hot
    target_slot = targets * CAP + jnp.sum(earlier * one_hot, -1)
    matches = target_slot[None, :] == jnp.arange(slots_total, dtype=jnp.int32)[:, None]
    filled = jnp.any(matches, 1).astype(jnp.int32)
    source = jnp.sum(
        matches.astype(jnp.int32) * jnp.arange(blocks, dtype=jnp.int32)[None, :], 1
    )

    chunks = []
    for chunk in CHUNKS:
        parts = product(rows_all, [held[k] for k in chunk])
        summed = [parts[0]]
        for step in range(1, Y):
            summed.append(lax.ppermute(parts[step], "tp", tp_pairs(0, step, 0)))
        away = sum(part[rows:].astype(F32) for part in summed).astype(BF16)
        summed.append(lax.ppermute(away, "tp", tp_pairs(1, 0, 0)))
        chunks.append(summed)

    outgoing = finish(column_of, source, filled, cosine, sine, scale, chunks, groups)
    result = lax.all_to_all(outgoing, "group", split_axis=0, concat_axis=0, tiled=True)
    return result.reshape(1, slots_total, tok, KVW)


def solution(mesh):
    in_specs = (
        P("group", None, None, "tp"),
        P("tp"),
        P("group", "tp", None),
        P("group", None),
        P("group", None),
        P("group", None),
    )
    out_specs = P("group", None, "tp", None)
    return jax.shard_map(body, mesh=mesh, in_specs=in_specs, out_specs=out_specs, check_vma=False)
```

time: 406 us -> 204 us (0.50); the launches traced: 401 us -> 204 us
  waiting for transfers between devices: 246 us -> 68.1 us
  starting transfers between devices: 20 us -> 54.3 us
  local copies, waits for them, and re-layouts: 38.3 us -> 18.7 us
  blocking collectives: 50.1 us -> 35.9 us
  matrix products: 14.2 us -> 0 us
  between operations: 13.6 us -> 0.37 us
  Pallas kernels: 0 us -> 8.02 us
    all_to_all x3 -> x0, waiting for transfers between devices: 119 us -> none  [the longest x1 99.9 us: body(): lax.all_to_all(outgoing, 'group', split_axis=0, concat_axis=0, tiled=True)]
    ppermute x0 -> x30, waiting for transfers between devices: none -> 68.1 us  [the longest x6 22.4 us: body(): summed.append(lax.ppermute(parts[step], 'tp', tp_pairs(0, step, 0)))]
    psum x1 -> x0, waiting for transfers between devices: 65.3 us -> none  [from_root(): return lax.psum(block, axis)]
    reduce_scatter x1 -> x0, waiting for transfers between devices: 61.3 us -> none  [body(): lax.psum_scatter(jnp.einsum('ncd,dk->cnk', normed, weights, preferred_ele...]
    ppermute x0 -> x30, starting transfers between devices: none -> 54.3 us  [the longest x6 19.9 us: body(): summed.append(lax.ppermute(parts[step], 'tp', tp_pairs(0, step, 0)))]
    psum x1 -> x0, blocking collectives: 50.1 us -> none  [body(): squares = lax.psum(jnp.sum(values * values, -1), 'tp')]
    all_to_all x0 -> x1, blocking collectives: none -> 35.9 us  [body(): lax.all_to_all(outgoing, 'group', split_axis=0, concat_axis=0, tiled=True)]
    convert_element_type x2 -> x1, local copies, waits for them, and re-layouts: 24.1 us -> 0.08 us  [body(): angles = positions.astype(F32)[:, None] * freqs]
  transfers between devices with their start and end apart: 5 -> 30, of which waited for: 5 -> 17; matrix products, arithmetic and copies ran while one was open for 4% -> 10% of each run, Pallas kernels for 0% -> 3%
where the time goes in v1:
time: 204 us
  waiting for transfers between devices  68.1 us (33%)
  starting transfers between devices  54.3 us (27%)
  blocking collectives  35.9 us (18%)
  local copies, waits for them, and re-layouts  18.7 us (9%)
  other arithmetic  18.2 us (9%)
  Pallas kernels  8.02 us (4%)
    all_to_all x1, blocking collectives, body(): lax.all_to_all(outgoing, 'group', split_axis=0, concat_axis=0, tiled=True)  35.9 us
    ppermute x6, waiting for transfers between devices, body(): summed.append(lax.ppermute(parts[step], 'tp', tp_pairs(0, step, 0)))  22.4 us
    ppermute x6, starting transfers between devices, body(): summed.append(lax.ppermute(parts[step], 'tp', tp_pairs(0, step, 0)))  19.9 us
    ppermute x7, starting transfers between devices, spread_weights(): own = own + lax.ppermute(pieces[k], 'group', [(0, 2 * k)])  19.1 us
    ppermute x3, waiting for transfers between devices, spread_weights(): moving = lax.ppermute(moving, ('group', 'tp'), ring_pairs())  15.9 us
    ppermute x7, waiting for transfers between devices, spread_weights(): own = own + lax.ppermute(pieces[k], 'group', [(0, 2 * k)])  14.7 us
    unnamed x47, local copies, waits for them, and re-layouts  12.5 us
    pallas_call x2, Pallas kernels, product(): pl.pallas_call(functools.partial(product_kernel, count), out_shape=[jax.S...  6.24 us
  transfers between devices with their start and end apart: 30, of which 17 were waited for; matrix products, arithmetic and copies ran while one was open for 10% of the time, Pallas kernels for 3%

profile of v1, /device:TPU:8, one launch (start us, length us, event | category | flops | bytes accessed | tf_op | source)
XLA Modules:
  0.0 203.6 jit_solution(14165434319480673921)
XLA Ops:
  0.8 2.5 %fusion = bf16[512,2048]{1,0:T(8,128)(2,1)S(1)} fusion(f32[512]{0:T(512)S(1)} %convert_element_type.75, f32[1,512,2048]{2,1,0:T(8,128)} %param.11), kind=kLoop, calls=%fused_computation.3 | loop fusion | flops 4194304 | bytes 6293504 | tf_op jit(solution)/shard_map/convert_element_type | solution.py:169
  5.8 8.5 %collective-permute-start.11 = (bf16[512,256]{1,0:T(8,128)(2,1)}, bf16[512,256]{1,0:T(8,128)(2,1)}, u32[]{:S(2)}, u32[]{:S(2)}) collective-permute-start(bf16[512,256]{1,0:T(8,128)(2,1)} %get-tuple-element.25), channel_id=1, source_target_pairs={{0,224},{1,225},{2,226},{3,227},{4,228},{5,229},{6,230},{7,231},{8... | collective-permute-start | bytes 786440 | tf_op jit(solution)/shard_map/ppermute | solution.py:131
  14.3 2.0 collective-permute-start.10
  16.3 2.0 collective-permute-start.9
  18.3 2.0 collective-permute-start.8
  20.3 2.0 collective-permute-start.7
  28.8 1.9 collective-permute-done.9
  32.2 5.6 %collective-permute-done.6 = bf16[512,256]{1,0:T(8,128)(2,1)S(1)} collective-permute-done((bf16[512,256]{1,0:T(8,128)(2,1)}, bf16[512,256]{1,0:T(8,128)(2,1)S(1)}, u32[]{:S(2)}, u32[]{:S(2)}) %collective-permute-start.6) | collective-permute-done | bytes 262176 | tf_op jit(solution)/shard_map/ppermute | solution.py:131
  37.8 4.4 %collective-permute-done.5 = bf16[512,256]{1,0:T(8,128)(2,1)S(1)} collective-permute-done((bf16[512,256]{1,0:T(8,128)(2,1)S(1)}, bf16[512,256]{1,0:T(8,128)(2,1)S(1)}, u32[]{:S(2)}, u32[]{:S(2)}) %collective-permute-start.5) | collective-permute-done | bytes 262176 | tf_op jit(solution)/shard_map/ppermute | solution.py:131
  45.0 4.8 %collective-permute-done.12 = bf16[512,256]{1,0:T(8,128)(2,1)S(1)} collective-permute-done((bf16[512,256]{1,0:T(8,128)(2,1)S(1)}, bf16[512,256]{1,0:T(8,128)(2,1)S(1)}, u32[]{:S(2)}, u32[]{:S(2)}) %collective-permute-start.12) | collective-permute-done | bytes 262176 | tf_op jit(solution)/shard_map/ppermute | solution.py:132
  51.7 2.6 %collective-permute-start.14 = (bf16[1024,256]{1,0:T(8,128)(2,1)S(1)}, bf16[1024,256]{1,0:T(8,128)(2,1)}, u32[]{:S(2)}, u32[]{:S(2)}) collective-permute-start(bf16[1024,256]{1,0:T(8,128)(2,1)S(1)} %pad_maximum_fusion.1.refs_0_), channel_id=1, source_target_pairs={{0,32},{1,225},{2,34},{3,227},{4,36},{5,229},{6,38},{7,231},{8,40}... | collective-permute-start | bytes 1572872 | tf_op jit(solution)/shard_map/ppermute | solution.py:139
  55.0 1.6 gather_fusion
  57.0 5.2 %collective-permute-done.14.refs_1_ = bf16[1024,256]{1,0:T(8,128)(2,1)} collective-permute-done((bf16[1024,256]{1,0:T(8,128)(2,1)S(1)}, bf16[1024,256]{1,0:T(8,128)(2,1)}, u32[]{:S(2)}, u32[]{:S(2)}) %collective-permute-start.14) | collective-permute-done | bytes 524320 | tf_op jit(solution)/shard_map/ppermute | solution.py:139
  63.6 9.3 %collective-permute-done.16.refs_3_ = bf16[1024,256]{1,0:T(8,128)(2,1)} collective-permute-done((bf16[1024,256]{1,0:T(8,128)(2,1)}, bf16[1024,256]{1,0:T(8,128)(2,1)}, u32[]{:S(2)}, u32[]{:S(2)}) %collective-permute-start.16) | collective-permute-done | bytes 524320 | tf_op jit(solution)/shard_map/ppermute | solution.py:139
  73.0 3.1 %broadcast_select_fusion.3 = (bf16[8,16,8,512]{3,2,1,0:T(8,128)(2,1)}, bf16[8,16,8,512]{3,2,1,0:T(8,128)(2,1)}) fusion(bf16[8,16,8,512]{3,2,1,0:T(8,128)(2,1)} %collective-permute-done, pred[]{:T(512)S(6)} %eq.44, bf16[8,16,8,512]{3,2,1,0:T(8,128)(2,1)} %gather_fusion, pred[8]{0:T(512)(128)(4,1)S(1)} %compare_and_fusion.1), kind=kLoop, calls=%fused_computation.9 | loop fusion | flops 1572864 | bytes 4194313 | tf_op jit(solution)/shard_map/jit(_where)/select_n | solution.py:179
  76.1 2.0 multiply_reduce_fusion
  79.4 2.7 %collective-permute-start.2 = (f32[2,128]{1,0:T(2,128)S(1)}, f32[2,128]{1,0:T(2,128)S(1)}, u32[]{:S(2)}, u32[]{:S(2)}) collective-permute-start(f32[2,128]{1,0:T(2,128)S(1)} %squeeze.22), channel_id=1, source_target_pairs={{0,4},{1,5},{2,6},{3,7},{4,0},{5,1},{6,2},{7,3},{8,12},{9,13},{10,... | collective-permute-start | bytes 3080 | tf_op jit(solution)/shard_map/ppermute | solution.py:185
  85.9 3.1 %pad_maximum_fusion = bf16[8,16,8,1024]{3,2,1,0:T(8,128)(2,1)} fusion(bf16[8,16,8,512]{3,2,1,0:T(8,128)(2,1)} %get-tuple-element.23, bf16[8,16,8,512]{3,2,1,0:T(8,128)(2,1)} %get-tuple-element.22), kind=kLoop, calls=%fused_computation.5 | loop fusion | flops 4194304 | bytes 4194304 | tf_op jit(solution)/shard_map/concatenate | solution.py:178
  89.1 4.6 %collective-permute-done.24 = bf16[512,256]{1,0:T(8,128)(2,1)} collective-permute-done((bf16[512,256]{1,0:T(8,128)(2,1)}, bf16[512,256]{1,0:T(8,128)(2,1)}, u32[]{:S(2)}, u32[]{:S(2)}) %collective-permute-start.24) | collective-permute-done | bytes 262176 | tf_op jit(solution)/shard_map/ppermute | solution.py:143
  93.8 1.6 copy-done.1
  95.4 4.4 %shard_map.73 = (bf16[256,1280]{1,0:T(8,128)(2,1)S(1)}, bf16[256,1280]{1,0:T(8,128)(2,1)S(1)}, bf16[256,1280]{1,0:T(8,128)(2,1)S(1)}, bf16[256,1280]{1,0:T(8,128)(2,1)S(1)}) custom-call(bf16[4,256,1024]{2,1,0:T(8,128)(2,1)S(1)} %bitcast.32, bf16[1024,256]{1,0:T(8,128)(2,1)S(1)} %pad_maximum_fusion.1.refs_0_, ...), custom_call_target="tpu_custom_call" | custom-call | flops 2684354560 | bytes 7340032 | tf_op jit(solution)/shard_map/pallas_call | solution.py:62
  103.6 1.6 collective-permute-start.4
  106.2 1.8 shard_map.74
  109.0 8.4 %collective-permute-done.18.refs_1_ = bf16[256,1280]{1,0:T(8,128)(2,1)S(1)} collective-permute-done((bf16[256,1280]{1,0:T(8,128)(2,1)S(1)}, bf16[256,1280]{1,0:T(8,128)(2,1)S(1)}, u32[]{:S(2)}, u32[]{:S(2)}) %collective-permute-start.18) | collective-permute-done | bytes 655392 | tf_op jit(solution)/shard_map/ppermute | solution.py:215
  118.4 1.9 collective-permute-done.19.refs_2_
  120.3 14.3 %collective-permute-start.28 = (bf16[256,768]{1,0:T(8,128)(2,1)S(1)}, bf16[256,768]{1,0:T(8,128)(2,1)S(1)}, u32[]{:S(2)}, u32[]{:S(2)}) collective-permute-start(bf16[256,768]{1,0:T(8,128)(2,1)S(1)} %get-tuple-element.21), channel_id=1, source_target_pairs={{0,6},{1,7},{2,0},{3,1},{4,2},{5,3},{6,4},{7,5},{8,14},{9,15},{10,... | collective-permute-start | bytes 1179656 | tf_op jit(solution)/shard_map/ppermute | solution.py:215
  137.9 2.0 %collective-permute-done.26.refs_6_ = bf16[256,768]{1,0:T(8,128)(2,1)S(1)} collective-permute-done((bf16[256,768]{1,0:T(8,128)(2,1)S(1)}, bf16[256,768]{1,0:T(8,128)(2,1)S(1)}, u32[]{:S(2)}, u32[]{:S(2)}) %collective-permute-start.26) | collective-permute-done | bytes 393248 | tf_op jit(solution)/shard_map/ppermute | solution.py:215
  140.0 2.9 %collective-permute-done.27.refs_7_ = bf16[256,768]{1,0:T(8,128)(2,1)S(1)} collective-permute-done((bf16[256,768]{1,0:T(8,128)(2,1)S(1)}, bf16[256,768]{1,0:T(8,128)(2,1)S(1)}, u32[]{:S(2)}, u32[]{:S(2)}) %collective-permute-start.27) | collective-permute-done | bytes 393248 | tf_op jit(solution)/shard_map/ppermute | solution.py:215
  142.9 7.1 %collective-permute-done.28.refs_8_ = bf16[256,768]{1,0:T(8,128)(2,1)S(1)} collective-permute-done((bf16[256,768]{1,0:T(8,128)(2,1)S(1)}, bf16[256,768]{1,0:T(8,128)(2,1)S(1)}, u32[]{:S(2)}, u32[]{:S(2)}) %collective-permute-start.28) | collective-permute-done | bytes 393248 | tf_op jit(solution)/shard_map/ppermute | solution.py:215
  153.7 4.2 %collective-permute-done.29.refs_9_ = bf16[128,768]{1,0:T(8,128)(2,1)} collective-permute-done((bf16[128,768]{1,0:T(8,128)(2,1)}, bf16[128,768]{1,0:T(8,128)(2,1)}, u32[]{:S(2)}, u32[]{:S(2)}) %collective-permute-start.29) | collective-permute-done | bytes 196640 | tf_op jit(solution)/shard_map/ppermute | solution.py:217
  164.9 1.8 shard_map.75
  166.7 35.9 %all_to_all.5 = bf16[16,16,2048]{2,1,0:T(8,128)(2,1)S(1)} all-to-all(bf16[16,16,2048]{2,1,0:T(8,128)(2,1)S(1)} %shard_map.75), channel_id=1, replica_groups=mesh['group'=16,'tp'=16] {'group'}, dimensions={0} | all-to-all | bytes 2097152 | tf_op jit(solution)/shard_map/all_to_all | solution.py:221
  (134 shorter events, 45.4 us)
Async XLA Ops:
  5.8 17.7 %collective-permute-start.11 = (bf16[512,256]{1,0:T(8,128)(2,1)}, bf16[512,256]{1,0:T(8,128)(2,1)}, u32[]{:S(2)}, u32[]{:S(2)}) collective-permute-start(bf16[512,256]{1,0:T(8,128)(2,1)} %get-tuple-element.25), channel_id=1, source_target_pairs={{0,224},{1,225},{2,226},{3,227},{4,228},{5,229},{6,230},{7,231},{8... | collective-permute-start | bytes 786440 | tf_op jit(solution)/shard_map/ppermute | solution.py:131
  14.3 11.9 %collective-permute-start.10 = (bf16[512,256]{1,0:T(8,128)(2,1)}, bf16[512,256]{1,0:T(8,128)(2,1)}, u32[]{:S(2)}, u32[]{:S(2)}) collective-permute-start(bf16[512,256]{1,0:T(8,128)(2,1)} %get-tuple-element.26), channel_id=1, source_target_pairs={{0,192},{1,193},{2,194},{3,195},{4,196},{5,197},{6,198},{7,199},{8... | collective-permute-start | bytes 786440 | tf_op jit(solution)/shard_map/ppermute | solution.py:131
  16.3 14.4 %collective-permute-start.9 = (bf16[512,256]{1,0:T(8,128)(2,1)}, bf16[512,256]{1,0:T(8,128)(2,1)}, u32[]{:S(2)}, u32[]{:S(2)}) collective-permute-start(bf16[512,256]{1,0:T(8,128)(2,1)} %get-tuple-element.27), channel_id=1, source_target_pairs={{0,160},{1,161},{2,162},{3,163},{4,164},{5,165},{6,166},{7,167},{8... | collective-permute-start | bytes 786440 | tf_op jit(solution)/shard_map/ppermute | solution.py:131
  18.3 12.4 %collective-permute-start.8 = (bf16[512,256]{1,0:T(8,128)(2,1)}, bf16[512,256]{1,0:T(8,128)(2,1)}, u32[]{:S(2)}, u32[]{:S(2)}) collective-permute-start(bf16[512,256]{1,0:T(8,128)(2,1)} %get-tuple-element.28), channel_id=1, source_target_pairs={{0,128},{1,129},{2,130},{3,131},{4,132},{5,133},{6,134},{7,135},{8... | collective-permute-start | bytes 786440 | tf_op jit(solution)/shard_map/ppermute | solution.py:131
  20.3 11.9 %collective-permute-start.7 = (bf16[512,256]{1,0:T(8,128)(2,1)}, bf16[512,256]{1,0:T(8,128)(2,1)}, u32[]{:S(2)}, u32[]{:S(2)}) collective-permute-start(bf16[512,256]{1,0:T(8,128)(2,1)} %get-tuple-element.29), channel_id=1, source_target_pairs={{0,96},{1,97},{2,98},{3,99},{4,100},{5,101},{6,102},{7,103},{8,104... | collective-permute-start | bytes 786440 | tf_op jit(solution)/shard_map/ppermute | solution.py:131
  23.6 14.3 %collective-permute-start.6 = (bf16[512,256]{1,0:T(8,128)(2,1)}, bf16[512,256]{1,0:T(8,128)(2,1)S(1)}, u32[]{:S(2)}, u32[]{:S(2)}) collective-permute-start(bf16[512,256]{1,0:T(8,128)(2,1)} %get-tuple-element.30), channel_id=1, source_target_pairs={{0,64},{1,65},{2,66},{3,67},{4,68},{5,69},{6,70},{7,71},{8,72},{9,... | collective-permute-start | bytes 786440 | tf_op jit(solution)/shard_map/ppermute | solution.py:131
  26.2 15.9 %collective-permute-start.5 = (bf16[512,256]{1,0:T(8,128)(2,1)S(1)}, bf16[512,256]{1,0:T(8,128)(2,1)S(1)}, u32[]{:S(2)}, u32[]{:S(2)}) collective-permute-start(bf16[512,256]{1,0:T(8,128)(2,1)S(1)} %get-tuple-element.24), channel_id=1, source_target_pairs={{0,32},{1,33},{2,34},{3,35},{4,36},{5,37},{6,38},{7,39},{8,40},{9,... | collective-permute-start | bytes 786440 | tf_op jit(solution)/shard_map/ppermute | solution.py:131
  30.7 42.3 %collective-permute-start = (bf16[8,16,8,512]{3,2,1,0:T(8,128)(2,1)}, bf16[8,16,8,512]{3,2,1,0:T(8,128)(2,1)}, u32[]{:S(2)}, u32[]{:S(2)}) collective-permute-start(bf16[8,16,8,512]{3,2,1,0:T(8,128)(2,1)} %broadcast_select_fusion), channel_id=1, source_target_pairs={{0,1},{1,0},{2,3},{3,2},{4,5},{5,4},{6,7},{7,6},{8,9},{9,8},{10,11... | collective-permute-start | bytes 3145736 | tf_op jit(solution)/shard_map/ppermute | solution.py:45
  43.6 6.3 %collective-permute-start.12 = (bf16[512,256]{1,0:T(8,128)(2,1)S(1)}, bf16[512,256]{1,0:T(8,128)(2,1)S(1)}, u32[]{:S(2)}, u32[]{:S(2)}) collective-permute-start(bf16[512,256]{1,0:T(8,128)(2,1)S(1)} %fusion.7), channel_id=1, source_target_pairs={{0,16},{32,48},{64,80},{96,112},{128,144},{160,176},{192,208},{224... | collective-permute-start | bytes 786440 | tf_op jit(solution)/shard_map/ppermute | solution.py:132
  50.0 1.6 collective-permute-start.13
  51.7 10.6 %collective-permute-start.14 = (bf16[1024,256]{1,0:T(8,128)(2,1)S(1)}, bf16[1024,256]{1,0:T(8,128)(2,1)}, u32[]{:S(2)}, u32[]{:S(2)}) collective-permute-start(bf16[1024,256]{1,0:T(8,128)(2,1)S(1)} %pad_maximum_fusion.1.refs_0_), channel_id=1, source_target_pairs={{0,32},{1,225},{2,34},{3,227},{4,36},{5,229},{6,38},{7,231},{8,40}... | collective-permute-start | bytes 1572872 | tf_op jit(solution)/shard_map/ppermute | solution.py:139
  62.3 10.7 %collective-permute-start.16 = (bf16[1024,256]{1,0:T(8,128)(2,1)}, bf16[1024,256]{1,0:T(8,128)(2,1)}, u32[]{:S(2)}, u32[]{:S(2)}) collective-permute-start(bf16[1024,256]{1,0:T(8,128)(2,1)} %collective-permute-done.14.refs_1_), channel_id=1, source_target_pairs={{0,32},{1,225},{2,34},{3,227},{4,36},{5,229},{6,38},{7,231},{8,40}... | collective-permute-start | bytes 1572872 | tf_op jit(solution)/shard_map/ppermute | solution.py:139
  73.0 10.6 %collective-permute-start.22 = (bf16[1024,256]{1,0:T(8,128)(2,1)}, bf16[1024,256]{1,0:T(8,128)(2,1)S(1)}, u32[]{:S(2)}, u32[]{:S(2)}) collective-permute-start(bf16[1024,256]{1,0:T(8,128)(2,1)} %collective-permute-done.16.refs_3_), channel_id=1, source_target_pairs={{0,32},{1,225},{2,34},{3,227},{4,36},{5,229},{6,38},{7,231},{8,40}... | collective-permute-start | bytes 1572872 | tf_op jit(solution)/shard_map/ppermute | solution.py:139
  78.1 15.7 %collective-permute-start.15 = (bf16[1024,256]{1,0:T(8,128)(2,1)}, bf16[1024,256]{1,0:T(8,128)(2,1)}, u32[]{:S(2)}, u32[]{:S(2)}) collective-permute-start(bf16[1024,256]{1,0:T(8,128)(2,1)} %collective-permute-done.14.refs_1_), channel_id=1, source_target_pairs={{0,1},{1,0},{2,3},{3,2},{4,5},{5,4},{6,7},{7,6},{8,9},{9,8},{10,11... | collective-permute-start | bytes 1572872 | tf_op jit(solution)/shard_map/ppermute | solution.py:45
  78.2 15.6 %collective-permute-start.17 = (bf16[1024,256]{1,0:T(8,128)(2,1)}, bf16[1024,256]{1,0:T(8,128)(2,1)}, u32[]{:S(2)}, u32[]{:S(2)}) collective-permute-start(bf16[1024,256]{1,0:T(8,128)(2,1)} %collective-permute-done.16.refs_3_), channel_id=1, source_target_pairs={{0,1},{1,0},{2,3},{3,2},{4,5},{5,4},{6,7},{7,6},{8,9},{9,8},{10,11... | collective-permute-start | bytes 1572872 | tf_op jit(solution)/shard_map/ppermute | solution.py:45
  78.8 7.1 %collective-permute-start.3 = (f32[2,128]{1,0:T(2,128)S(1)}, f32[2,128]{1,0:T(2,128)S(1)}, u32[]{:S(2)}, u32[]{:S(2)}) collective-permute-start(f32[2,128]{1,0:T(2,128)S(1)} %squeeze.23), channel_id=1, source_target_pairs={{0,6},{1,7},{2,0},{3,1},{4,2},{5,3},{6,4},{7,5},{8,14},{9,15},{10,... | collective-permute-start | bytes 3080 | tf_op jit(solution)/shard_map/ppermute | solution.py:185
  79.4 9.7 %collective-permute-start.2 = (f32[2,128]{1,0:T(2,128)S(1)}, f32[2,128]{1,0:T(2,128)S(1)}, u32[]{:S(2)}, u32[]{:S(2)}) collective-permute-start(f32[2,128]{1,0:T(2,128)S(1)} %squeeze.22), channel_id=1, source_target_pairs={{0,4},{1,5},{2,6},{3,7},{4,0},{5,1},{6,2},{7,3},{8,12},{9,13},{10,... | collective-permute-start | bytes 3080 | tf_op jit(solution)/shard_map/ppermute | solution.py:185
  83.6 5.6 %collective-permute-start.1 = (f32[2,128]{1,0:T(2,128)S(1)}, f32[2,128]{1,0:T(2,128)S(1)}, u32[]{:S(2)}, u32[]{:S(2)}) collective-permute-start(f32[2,128]{1,0:T(2,128)S(1)} %squeeze.21), channel_id=1, source_target_pairs={{0,2},{1,3},{2,4},{3,5},{4,6},{5,7},{6,0},{7,1},{8,10},{9,11},{10,... | collective-permute-start | bytes 3080 | tf_op jit(solution)/shard_map/ppermute | solution.py:185
  85.9 7.9 %collective-permute-start.24 = (bf16[512,256]{1,0:T(8,128)(2,1)}, bf16[512,256]{1,0:T(8,128)(2,1)}, u32[]{:S(2)}, u32[]{:S(2)}) collective-permute-start(bf16[512,256]{1,0:T(8,128)(2,1)} %constant_dynamic-slice_fusion), channel_id=1, source_target_pairs={{0,32},{1,225},{2,34},{3,227},{4,36},{5,229},{6,38},{7,231},{8,40}... | collective-permute-start | bytes 786440 | tf_op jit(solution)/shard_map/ppermute | solution.py:143
  93.8 9.8 %collective-permute-start.25 = (bf16[512,256]{1,0:T(8,128)(2,1)}, bf16[512,256]{1,0:T(8,128)(2,1)S(1)}, u32[]{:S(2)}, u32[]{:S(2)}) collective-permute-start(bf16[512,256]{1,0:T(8,128)(2,1)} %collective-permute-done.24), channel_id=1, source_target_pairs={{0,1},{1,0},{2,3},{3,2},{4,5},{5,4},{6,7},{7,6},{8,9},{9,8},{10,11... | collective-permute-start | bytes 786440 | tf_op jit(solution)/shard_map/ppermute | solution.py:45
  99.9 17.6 %collective-permute-start.18 = (bf16[256,1280]{1,0:T(8,128)(2,1)S(1)}, bf16[256,1280]{1,0:T(8,128)(2,1)S(1)}, u32[]{:S(2)}, u32[]{:S(2)}) collective-permute-start(bf16[256,1280]{1,0:T(8,128)(2,1)S(1)} %get-tuple-element.15), channel_id=1, source_target_pairs={{0,2},{1,3},{2,4},{3,5},{4,6},{5,7},{6,0},{7,1},{8,10},{9,11},{10,... | collective-permute-start | bytes 1966088 | tf_op jit(solution)/shard_map/ppermute | solution.py:215
  101.2 19.1 %collective-permute-start.19 = (bf16[256,1280]{1,0:T(8,128)(2,1)S(1)}, bf16[256,1280]{1,0:T(8,128)(2,1)S(1)}, u32[]{:S(2)}, u32[]{:S(2)}) collective-permute-start(bf16[256,1280]{1,0:T(8,128)(2,1)S(1)} %get-tuple-element.16), channel_id=1, source_target_pairs={{0,4},{1,5},{2,6},{3,7},{4,0},{5,1},{6,2},{7,3},{8,12},{9,13},{10,... | collective-permute-start | bytes 1966088 | tf_op jit(solution)/shard_map/ppermute | solution.py:215
  102.5 32.2 %collective-permute-start.20 = (bf16[256,1280]{1,0:T(8,128)(2,1)S(1)}, bf16[256,1280]{1,0:T(8,128)(2,1)S(1)}, u32[]{:S(2)}, u32[]{:S(2)}) collective-permute-start(bf16[256,1280]{1,0:T(8,128)(2,1)S(1)} %get-tuple-element.17), channel_id=1, source_target_pairs={{0,6},{1,7},{2,0},{3,1},{4,2},{5,3},{6,4},{7,5},{8,14},{9,15},{10,... | collective-permute-start | bytes 1966088 | tf_op jit(solution)/shard_map/ppermute | solution.py:215
  103.5 2.6 %collective-permute-start.23 = (bf16[1024,256]{1,0:T(8,128)(2,1)S(1)}, bf16[1024,256]{1,0:T(8,128)(2,1)S(1)}, u32[]{:S(2)}, u32[]{:S(2)}) collective-permute-start(bf16[1024,256]{1,0:T(8,128)(2,1)S(1)} %copy-done.16), channel_id=1, source_target_pairs={{0,1},{1,0},{2,3},{3,2},{4,5},{5,4},{6,7},{7,6},{8,9},{9,8},{10,11... | collective-permute-start | bytes 1572872 | tf_op jit(solution)/shard_map/ppermute | solution.py:45
  103.6 49.4 %collective-permute-start.4 = (f32[128]{0:T(128)S(1)}, f32[128]{0:T(128)S(1)}, u32[]{:S(2)}, u32[]{:S(2)}) collective-permute-start(f32[128]{0:T(128)S(1)} %slice_bitcast_fusion), channel_id=1, source_target_pairs={{0,8},{1,9},{2,10},{3,11},{4,12},{5,13},{6,14},{7,15},{8,0},{9,1},... | collective-permute-start | bytes 1544 | tf_op jit(solution)/shard_map/ppermute | solution.py:186
  108.0 42.0 %copy-start.6 = (bf16[256,768]{1,0:T(8,128)(2,1)}, bf16[256,768]{1,0:T(8,128)(2,1)S(1)}, u32[]{:S(2)}) copy-start(bf16[256,768]{1,0:T(8,128)(2,1)S(1)} %get-tuple-element.18.refs_5_) | copy-start | bytes 1179652
  108.0 45.0 %copy-start.19 = (pred[128]{0:T(512)(128)(4,1)S(1)}, pred[128]{0:T(512)(128)(4,1)}, u32[]{:S(2)}) copy-start(pred[128]{0:T(512)(128)(4,1)} %lt.50) | copy-start | bytes 388
  108.0 32.0 %collective-permute-start.26 = (bf16[256,768]{1,0:T(8,128)(2,1)S(1)}, bf16[256,768]{1,0:T(8,128)(2,1)S(1)}, u32[]{:S(2)}, u32[]{:S(2)}) collective-permute-start(bf16[256,768]{1,0:T(8,128)(2,1)S(1)} %get-tuple-element.19), channel_id=1, source_target_pairs={{0,2},{1,3},{2,4},{3,5},{4,6},{5,7},{6,0},{7,1},{8,10},{9,11},{10,... | collective-permute-start | bytes 1179656 | tf_op jit(solution)/shard_map/ppermute | solution.py:215
  117.5 25.4 %collective-permute-start.27 = (bf16[256,768]{1,0:T(8,128)(2,1)S(1)}, bf16[256,768]{1,0:T(8,128)(2,1)S(1)}, u32[]{:S(2)}, u32[]{:S(2)}) collective-permute-start(bf16[256,768]{1,0:T(8,128)(2,1)S(1)} %get-tuple-element.20), channel_id=1, source_target_pairs={{0,4},{1,5},{2,6},{3,7},{4,0},{5,1},{6,2},{7,3},{8,12},{9,13},{10,... | collective-permute-start | bytes 1179656 | tf_op jit(solution)/shard_map/ppermute | solution.py:215
  120.3 29.6 %collective-permute-start.28 = (bf16[256,768]{1,0:T(8,128)(2,1)S(1)}, bf16[256,768]{1,0:T(8,128)(2,1)S(1)}, u32[]{:S(2)}, u32[]{:S(2)}) collective-permute-start(bf16[256,768]{1,0:T(8,128)(2,1)S(1)} %get-tuple-element.21), channel_id=1, source_target_pairs={{0,6},{1,7},{2,0},{3,1},{4,2},{5,3},{6,4},{7,5},{8,14},{9,15},{10,... | collective-permute-start | bytes 1179656 | tf_op jit(solution)/shard_map/ppermute | solution.py:215
  136.4 17.3 %collective-permute-start.21 = (bf16[128,1280]{1,0:T(8,128)(2,1)}, bf16[128,1280]{1,0:T(8,128)(2,1)}, u32[]{:S(2)}, u32[]{:S(2)}) collective-permute-start(bf16[128,1280]{1,0:T(8,128)(2,1)} %add_convert_fusion), channel_id=1, source_target_pairs={{0,8},{1,9},{2,10},{3,11},{4,12},{5,13},{6,14},{7,15},{8,0},{9,1},... | collective-permute-start | bytes 983048 | tf_op jit(solution)/shard_map/ppermute | solution.py:217
  151.5 6.5 %collective-permute-start.29 = (bf16[128,768]{1,0:T(8,128)(2,1)}, bf16[128,768]{1,0:T(8,128)(2,1)}, u32[]{:S(2)}, u32[]{:S(2)}) collective-permute-start(bf16[128,768]{1,0:T(8,128)(2,1)} %add_convert_fusion.1), channel_id=1, source_target_pairs={{0,8},{1,9},{2,10},{3,11},{4,12},{5,13},{6,14},{7,15},{8,0},{9,1},... | collective-permute-start | bytes 589832 | tf_op jit(solution)/shard_map/ppermute | solution.py:217
  (21 other events, 136.5 us)

commit v2 on v0

v2 whole, which is shorter than its diff:
```python
import functools

import jax
import jax.numpy as jnp
from jax import lax
from jax.experimental import pallas as pl
from jax.experimental.pallas import tpu as pltpu
from jax.sharding import PartitionSpec as P

D = 8192
HEAD = 128
BLOCK = 128
CAP = 2
KVW = 2048
Z = 8
X = 2
Y = 4
PIECES = 8
EARLY = 10
EXTRA = 16
BF16 = jnp.bfloat16
F32 = jnp.float32
I32 = jnp.int32
VMEM = pl.BlockSpec(memory_space=pltpu.VMEM)
SMEM = pl.BlockSpec(memory_space=pltpu.SMEM)
ANY = pl.BlockSpec(memory_space=pl.ANY)
HBM = pl.BlockSpec(memory_space=pltpu.HBM)


def tp_pairs(dx, dy, dc):
    pairs = []
    for t in range(16):
        x, y, c = t // 8, (t // 2) % 4, t % 2
        pairs.append((t, ((x ^ dx) * 4 + (y + dy) % Y) * 2 + (c ^ dc)))
    return pairs


def ring_pairs(cores):
    pairs = []
    for g in range(16):
        for t in range(16):
            z, h, c = g // 2, g % 2, t % 2
            there = (z + (1 if c == 0 else -1)) % Z
            if c in cores:
                pairs.append((g * 16 + t, (there * 2 + h) * 16 + t))
    return pairs


def to_core(value):
    return lax.ppermute(value, "tp", tp_pairs(0, 0, 1))


def load(sources, targets, sem, first=0):
    copies = [
        pltpu.make_async_copy(source, target, sem.at[first + n])
        for n, (source, target) in enumerate(zip(sources, targets, strict=True))
    ]
    for copy in copies:
        copy.start()
    return copies


def wait(copies):
    for copy in copies:
        copy.wait()


def buffers(shapes, count):
    return [pltpu.VMEM(shape, dtype) for shape, dtype in shapes] + [pltpu.SemaphoreType.DMA((count,))]


def like(arrays):
    return [(array.shape, array.dtype) for array in arrays]


def params(mib):
    return pltpu.CompilerParams(vmem_limit_bytes=mib * 2**20)


def weights_kernel(gain_ref, weights_ref, *outs):
    rows = weights_ref.shape[0]
    gain = gain_ref[...].astype(F32)
    down = lax.broadcasted_iota(I32, (rows, rows), 0)
    across = lax.broadcasted_iota(I32, (rows, rows), 1)
    gain = jnp.sum(jnp.where(down == across, gain, 0.0), 1, keepdims=True)
    for k, out in enumerate(outs):
        for half in range(2):
            first = half * (KVW // 2) + k * HEAD
            part = weights_ref[:, first : first + HEAD].astype(BF16).astype(F32)
            out[half] = (part * gain).astype(BF16)


def weight_pieces(gain, weights):
    features, step = weights.shape[0], 256
    return pl.pallas_call(
        weights_kernel,
        grid=(features // step,),
        out_shape=[jax.ShapeDtypeStruct((2, features, HEAD), BF16)] * PIECES,
        in_specs=[
            pl.BlockSpec((1, step), lambda i: (0, i)),
            pl.BlockSpec((step, KVW), lambda i: (i, 0)),
        ],
        out_specs=[pl.BlockSpec((2, step, HEAD), lambda i: (0, i, 0))] * PIECES,
        compiler_params=pltpu.CompilerParams(vmem_limit_bytes=60 * 2**20),
    )(gain[None, :], weights)


def combine_kernel(learner_ref, *refs):
    pieces, out, (held, sem) = refs[:PIECES], refs[-3], refs[-2:]
    copies = load(pieces, [held.at[k] for k in range(PIECES)], sem)
    wait(copies)
    total = jnp.where(learner_ref[0] > 0, held[0], jnp.zeros_like(held[0]))
    for k in range(1, PIECES):
        total = total + held[k]
    held[0] = total
    wait(load([held.at[0]], [out], sem))


def combine(learner, pieces, others):
    shape = pieces[0].shape
    return pl.pallas_call(
        combine_kernel,
        out_shape=jax.ShapeDtypeStruct(shape, BF16),
        in_specs=[SMEM] + [HBM] * PIECES + [ANY] * len(others),
        out_specs=HBM,
        scratch_shapes=buffers([((PIECES,) + shape, BF16)], PIECES),
        compiler_params=params(60),
    )(learner, *pieces, *others)


def spread_weights(pieces, group, x, others):
    z = group // 2
    arrived = [lax.ppermute(pieces[k], "group", [(0, 2 * k)]) for k in (4, 5, 3, 6, 2, 7, 1)]
    learner = (group == 0).astype(I32)[None]
    own = combine(learner, [pieces[0]] + arrived, others)
    own = own + lax.ppermute(own, "group", [(2 * k, 2 * k + 1) for k in range(Z)])
    first = x == 0
    same, other = jnp.where(first, own[0], own[1]), jnp.where(first, own[1], own[0])
    arrived = over_x(other)
    diagonal = lax.ppermute(other, "tp", tp_pairs(1, 0, 1))
    held = [jnp.concatenate([same, to_core(same), arrived, diagonal], 0)]
    for step in range(1, 4):
        held.append(lax.ppermute(held[-1], ("group", "tp"), ring_pairs((0, 1))))
    return held, arrived


def product_kernel(count, extra, where_ref, *refs):
    tokens, pieces = refs[:6], refs[6 : 6 + count]
    results, (rows, thin, wide, held, sem) = refs[-5 - Y : -5], refs[-5:]
    features = rows.shape[-1]
    weights = load(pieces, [thin.at[k] for k in range(count)], sem)
    copies = []
    for dy in range(Y):
        owner = lax.rem(where_ref[0] + dy, Y)
        sources = [token.at[:, :, owner] for token in tokens]
        targets = [rows.at[dy, 0], rows.at[dy, 1]]
        for n in (2, 3):
            targets += [rows.at[dy, n, :EARLY], rows.at[dy, n, EARLY:]]
        copies.append(load(sources, targets, sem, count + 6 * dy))
    wait(weights)
    first = where_ref[1] == 0
    for k in range(count - 1):
        wide[:, k * HEAD : (k + 1) * HEAD] = jnp.where(first, thin[k], thin[k + 1])
    out = []
    for dy in range(Y):
        wait(copies[dy])
        total = None
        for n in range(4):
            term = jnp.dot(
                rows[dy, n].reshape(-1, features),
                wide[n * features : (n + 1) * features, :],
                preferred_element_type=F32,
            )
            total = term if total is None else total + term
        held[dy, : total.shape[0], :] = total.astype(BF16)
        if extra:
            held[dy, total.shape[0] :, :] = refs[6 + count][dy]
        out += load([held.at[dy]], [results[dy]], sem, dy)
    wait(out)


def product(where, tokens, pieces, lines=(), others=()):
    count = len(pieces)
    blocks, tok, features = tokens[0].shape[0], tokens[0].shape[3], tokens[0].shape[4]
    rows = blocks * X * tok
    sent = rows + EXTRA * len(lines)
    depth, width = pieces[0].shape[0], (count - 1) * HEAD
    return pl.pallas_call(
        functools.partial(product_kernel, count, len(lines)),
        out_shape=[jax.ShapeDtypeStruct((sent, width), BF16)] * Y,
        in_specs=[SMEM] + [HBM] * (6 + count) + [VMEM] * len(lines) + [ANY] * len(others),
        out_specs=[HBM] * Y,
        scratch_shapes=buffers(
            [
                ((Y, 4, blocks, X, tok, features), BF16),
                ((count, depth, HEAD), BF16),
                ((depth, width), BF16),
                ((Y, sent, width), BF16),
            ],
            count + 6 * Y,
        ),
        compiler_params=params(60),
        cost_estimate=pl.CostEstimate(
            flops=2 * Y * rows * width * depth,
            bytes_accessed=2 * (Y * rows * depth + width * depth + Y * rows * width),
            transcendentals=0,
        ),
    )(where, *tokens, *pieces, *lines, *others)


def add_kernel(*refs):
    parts, out, (held, total, sem) = refs[:Y], refs[Y], refs[-3:]
    wait(load(parts, [held.at[n] for n in range(Y)], sem))
    total[...] = sum(held[n].astype(F32) for n in range(Y))
    wait(load([total], [out], sem))


def add(parts):
    shape = parts[0].shape
    return pl.pallas_call(
        add_kernel,
        out_shape=jax.ShapeDtypeStruct(shape, F32),
        in_specs=[HBM] * Y,
        out_specs=HBM,
        scratch_shapes=buffers([((Y,) + shape, BF16), (shape, F32)], Y),
        compiler_params=params(60),
    )(*parts)


def share_kernel(where_ref, summed_ref, *refs):
    parts, results, (summed, held, both, sent, line, sem) = refs[:Y], refs[Y : Y + 5], refs[-6:]
    copies = load(parts, [held.at[n] for n in range(Y)], sem)
    copies += load([summed_ref], [summed], sem, Y)
    wait(copies)
    width = summed.shape[-1]
    rows = summed.shape[0] - EXTRA
    both[..., :width] = summed[:rows].reshape(both.shape[:-1] + (width,))
    late = sum(held[n].astype(F32) for n in range(Y))
    both[..., width:] = late.reshape(both.shape[:-1] + (width,))
    total = summed[rows : rows + 2] + summed[rows + 2 : rows + 4]
    line[...] = total
    high = total.astype(BF16).astype(F32)
    extra = jnp.concatenate([high, total - high], 1)
    extra = jnp.concatenate([extra, jnp.zeros((EXTRA - 2, 2 * width), F32)], 0)
    x, core = where_ref[2], where_ref[1]
    copies = load([line], [results[4]], sem, 4)
    for n in (3, 2, 1, 0):
        chip = x if n < 2 else 1 - x
        of_core = core if n % 2 == 0 else 1 - core
        value = both[:, chip, of_core].reshape(-1, 2 * width)
        size = value.shape[0]
        sent[n, :size] = value.astype(BF16)
        if n == 2:
            sent[n, size:] = extra.astype(BF16)
            size += EXTRA
        copies += load([sent.at[n, :size]], [results[n]], sem, n)
    wait(copies)


def share(where, summed, parts, blocks, tok):
    width = 2 * summed.shape[1]
    rows = [blocks * tok + (EXTRA if n == 2 else 0) for n in range(4)]
    return pl.pallas_call(
        share_kernel,
        out_shape=[jax.ShapeDtypeStruct((each, width), BF16) for each in rows]
        + [jax.ShapeDtypeStruct((2, width // 2), F32)],
        in_specs=[SMEM] + [HBM] * (1 + Y),
        out_specs=[HBM] * 5,
        scratch_shapes=buffers(
            [
                (summed.shape, F32),
                ((Y,) + parts[0].shape, BF16),
                ((blocks, X, 2, tok, width), F32),
                ((4, rows[2], width), BF16),
                ((2, width // 2), F32),
            ],
            Y + 1,
        ),
        compiler_params=params(60),
    )(where, summed, *parts)


def after(values, others):
    count = len(values)
    return pl.pallas_call(
        lambda *refs: None,
        out_shape=[jax.ShapeDtypeStruct(value.shape, value.dtype) for value in values],
        in_specs=[ANY] * (count + len(others)),
        out_specs=[ANY] * count,
        input_output_aliases={i: i for i in range(count)},
    )(*values, *others)


def over_y(parts):
    return [parts[0]] + [
        lax.ppermute(parts[step], "tp", tp_pairs(0, step, 0)) for step in range(1, Y)
    ]


def over_x(value):
    return lax.ppermute(value, "tp", tp_pairs(1, 0, 0))


def squares_kernel(where_ref, mine_ref, theirs_ref, out, mine, theirs, sem):
    features = mine.shape[-1]
    wait(load([mine_ref, theirs_ref], [mine, theirs], sem))
    step = 128
    down = lax.broadcasted_iota(I32, (step, step), 0)
    across = lax.broadcasted_iota(I32, (step, step), 1)
    for dy in range(Y):
        owner = lax.rem(where_ref[0] + dy, Y)
        total = 0.0
        for token in (mine, theirs):
            rows = token[:, :, owner].reshape(-1, features).astype(F32)
            total = total + jnp.sum(rows * rows, 1, keepdims=True)
        lines = []
        for at in range(0, total.shape[0], step):
            turned = jnp.where(down == across, total[at : at + step], 0.0)
            lines.append(jnp.sum(turned, 0, keepdims=True))
        half = len(lines) // 2
        lines = [jnp.concatenate(lines[:half], 1), jnp.concatenate(lines[half:], 1)]
        lines = jnp.concatenate(lines, 0)
        high = lines.astype(BF16).astype(F32)
        rest = jnp.zeros((EXTRA - 4, lines.shape[1]), F32)
        out[dy] = jnp.concatenate([high, lines - high, rest], 0).astype(BF16)


def sums_of_squares(where, mine, theirs):
    rows = mine.shape[0] * X * mine.shape[3]
    return pl.pallas_call(
        squares_kernel,
        out_shape=jax.ShapeDtypeStruct((Y, EXTRA, rows // 2), BF16),
        in_specs=[SMEM] + [HBM] * 2,
        out_specs=VMEM,
        scratch_shapes=buffers(like([mine, theirs]), 2),
        compiler_params=params(60),
    )(where, mine, theirs)


def cut_kernel(begin, end, tokens_ref, *refs):
    out, held, sem = refs[-3:]
    wait(load([tokens_ref.at[begin:end]], [held], sem))
    wait(load([held], [out], sem))


def cut(tokens, begin, end, others=()):
    shape = (end - begin,) + tokens.shape[1:]
    return pl.pallas_call(
        functools.partial(cut_kernel, begin, end),
        out_shape=jax.ShapeDtypeStruct(shape, BF16),
        in_specs=[HBM] + [ANY] * len(others),
        out_specs=HBM,
        scratch_shapes=buffers([(shape, BF16)], 1),
        compiler_params=params(60),
    )(tokens, *others)


def finish_kernel(where_ref, source_ref, filled_ref, lines_ref, live_ref, cos_ref, sin_ref, *refs):
    sources, result, out_ref, done, parts, sem = refs[:4], refs[4], refs[5], refs[6], refs[7:11], refs[11]
    wait(load(sources, parts, sem))
    rows = cos_ref.shape[1]
    width = lines_ref.shape[1]
    arrived = parts[2][rows : rows + 2].astype(F32)
    total = lines_ref[...] + arrived[:, :width] + arrived[:, width:]
    inverse = lax.rsqrt(total / D + 1e-05)
    row = lax.broadcasted_iota(I32, (rows, width), 0)
    at = lax.broadcasted_iota(I32, (rows, width), 1)
    half = rows // 2
    tok = 8
    wanted = (row % half // tok) * 4 * tok + (where_ref[2] * 2 + where_ref[1]) * tok + row % tok
    lines = jnp.where(row < half, inverse[:1], inverse[1:])
    scale = jnp.sum(jnp.where(at == wanted, lines, 0.0), 1, keepdims=True)
    scale = jnp.where(live_ref[...] > 0, scale, 0.0)
    z, core, x = where_ref[3], where_ref[1], where_ref[2]
    for n, part in enumerate(parts):
        kind = x if n < 2 else 1 - x
        of_core = core if n % 2 == 0 else 1 - core
        for k in range(part.shape[1] // HEAD):
            value = part[:rows, k * HEAD : (k + 1) * HEAD].astype(F32) * scale
            other = pltpu.roll(value, HEAD // 2, 1)
            head = lax.rem(jnp.where(of_core == 0, z + PIECES - k, z + 1 + k), PIECES)
            start = pl.multiple_of((kind * PIECES + head) * HEAD, HEAD)
            done[:, pl.ds(start, HEAD)] = value * cos_ref[kind] + other * sin_ref[kind]
    copies = []
    for group in range(out_ref.shape[0]):
        both = []
        for j in range(group * CAP, (group + 1) * CAP):
            first = pl.multiple_of(source_ref[j] * tok, tok)
            both.append(jnp.where(filled_ref[j] > 0, done[pl.ds(first, tok), :], 0.0))
        out_ref[group] = jnp.concatenate(both, 0).astype(BF16)
        if group % 4 == 3:
            some = pl.ds(group - 3, 4)
            copies += load([out_ref.at[some]], [result.at[some]], sem, group // 4)
    wait(copies)


def finish(where, source, filled, lines, live, cosine, sine, parts, groups):
    shape = (groups, CAP * 8, KVW)
    return pl.pallas_call(
        finish_kernel,
        out_shape=jax.ShapeDtypeStruct(shape, BF16),
        in_specs=[SMEM] * 3 + [VMEM] * 4 + [HBM] * len(parts),
        out_specs=HBM,
        scratch_shapes=buffers(
            [(shape, BF16), ((cosine.shape[1], KVW), F32), *like(parts)], len(parts)
        ),
        compiler_params=params(60),
    )(where, source, filled, lines, live, cosine, sine, *parts)


def slots_of(plan, groups):
    blocks = plan.shape[0]
    one_hot = (plan[:, None] == jnp.arange(groups, dtype=I32)[None, :]).astype(I32)
    earlier = jnp.cumsum(one_hot, 0) - one_hot
    target_slot = plan * CAP + jnp.sum(earlier * one_hot, -1)
    matches = target_slot[None, :] == jnp.arange(groups * CAP, dtype=I32)[:, None]
    filled = jnp.any(matches, 1).astype(I32)
    source = jnp.sum(matches.astype(I32) * jnp.arange(blocks, dtype=I32)[None, :], 1)
    return source, filled


def body(hidden, norm_gain, learner_weights, plan, block_fill, block_pos):
    groups = lax.axis_size("group")
    blocks = hidden.shape[1]
    features = hidden.shape[3]
    group = lax.axis_index("group")
    tp = lax.axis_index("tp")
    x, y, core = tp // 8, (tp // 2) % Y, tp % 2
    tok = BLOCK // 16
    rows = blocks * tok

    pieces = weight_pieces(norm_gain, learner_weights[0])

    where = jnp.stack([y, core, x, group // 2]).astype(I32)
    mine = hidden[0].reshape(blocks, X, Y, 2 * tok, features)
    theirs = to_core(mine)
    early = over_x(cut(mine, 0, EARLY))
    late = cut(mine, EARLY, blocks, [pieces[0]])
    squares = sums_of_squares(where, mine, theirs)
    held, arrived = spread_weights(pieces, group, x, [early, late, squares])
    (late,) = after([late], [arrived])
    late = over_x(late)
    tokens = [mine, theirs, early, late, to_core(early), to_core(late)]

    first_parts = product(where, tokens, held[:3], [squares])
    (held[3],) = after([held[3]], [first_parts[1]])
    held.append(lax.ppermute(held[3], ("group", "tp"), ring_pairs((1,))))
    first_parts = over_y(first_parts)
    second_parts = over_y(product(where, tokens, held[2:], [], [first_parts[1]]))
    kept, *away, lines = share(where, add(first_parts), second_parts, blocks, tok)
    parts = [kept, to_core(away[0]), over_x(away[1])]
    parts.append(lax.ppermute(away[2], "tp", tp_pairs(1, 0, 1)))

    token = tp * tok + jnp.arange(tok, dtype=I32)
    positions = (block_pos[0][:, None] * BLOCK + token).reshape(rows)
    live = (token < block_fill[0][:, None]).reshape(rows, 1).astype(F32)
    half_width = HEAD // 2
    freqs = 500000.0 ** (-(jnp.arange(half_width, dtype=F32) * 2.0) / HEAD)
    angles = positions.astype(F32)[:, None] * freqs
    cosine, sine = jnp.cos(angles), jnp.sin(angles)
    cosine = jnp.concatenate([cosine, cosine], -1)
    sine = jnp.concatenate([-sine, sine], -1)
    cosine = jnp.stack([cosine, jnp.ones_like(cosine)])
    sine = jnp.stack([sine, jnp.zeros_like(sine)])
    source, filled = slots_of(plan[0], groups)

    outgoing = finish(where, source, filled, lines, live, cosine, sine, parts, groups)
    got = lax.all_to_all(outgoing, "group", split_axis=0, concat_axis=0, tiled=True)
    return got.reshape(1, groups * CAP, tok, KVW)


def solution(mesh):
    in_specs = (
        P("group", None, None, "tp"),
        P("tp"),
        P("group", "tp", None),
        P("group", None),
        P("group", None),
        P("group", None),
    )
    out_specs = P("group", None, "tp", None)
    return jax.shard_map(body, mesh=mesh, in_specs=in_specs, out_specs=out_specs, check_vma=False)
```

time: 406 us -> 188 us (0.46)
  waiting for transfers between devices: 246 us -> 41.5 us
  Pallas kernels: 0 us -> 41 us
  starting transfers between devices: 20 us -> 50.1 us
  local copies, waits for them, and re-layouts: 38.3 us -> 10.2 us
  other arithmetic: 19.4 us -> 4.72 us
  matrix products: 14.2 us -> 0 us
  between operations: 13.6 us -> 0.39 us
  blocking collectives: 50.1 us -> 39.3 us
    all_to_all x3 -> x0, waiting for transfers between devices: 119 us -> none  [the longest x1 99.9 us: body(): lax.all_to_all(outgoing, 'group', split_axis=0, concat_axis=0, tiled=True)]
    psum x1 -> x0, waiting for transfers between devices: 65.3 us -> none  [from_root(): return lax.psum(block, axis)]
    reduce_scatter x1 -> x0, waiting for transfers between devices: 61.3 us -> none  [body(): lax.psum_scatter(jnp.einsum('ncd,dk->cnk', normed, weights, preferred_ele...]
    psum x1 -> x0, blocking collectives: 50.1 us -> none  [body(): squares = lax.psum(jnp.sum(values * values, -1), 'tp')]
    ppermute x0 -> x29, starting transfers between devices: none -> 50.1 us  [the longest x7 19.7 us: spread_weights(): lax.ppermute(pieces[k], 'group', [(0, 2 * k)])]
    ppermute x0 -> x29, waiting for transfers between devices: none -> 41.5 us  [the longest x3 10.9 us: spread_weights(): held.append(lax.ppermute(held[-1], ('group', 'tp'), ring_pairs((0, 1))))]
    pallas_call x0 -> x12, Pallas kernels: none -> 41 us  [the longest x2 17.2 us: product(): pl.pallas_call(functools.partial(product_kernel, count, len(lines)), out_...]
    all_to_all x0 -> x1, blocking collectives: none -> 39.3 us  [body(): lax.all_to_all(outgoing, 'group', split_axis=0, concat_axis=0, tiled=True)]
  transfers between devices with their start and end apart: 5 -> 29, of which waited for: 5 -> 12; matrix products, arithmetic and copies ran while one was open for 4% -> 3% of each run, Pallas kernels for 0% -> 17%
where the time goes in v2:
time: 188 us; the launch traced here: 187 us
  starting transfers between devices  50.1 us (27%)
  waiting for transfers between devices  41.5 us (22%)
  Pallas kernels  41 us (22%)
  blocking collectives  39.3 us (21%)
  local copies, waits for them, and re-layouts  10.2 us (5%)
  other arithmetic  4.72 us (3%)
    all_to_all x1, blocking collectives, body(): lax.all_to_all(outgoing, 'group', split_axis=0, concat_axis=0, tiled=True)  39.3 us
    ppermute x7, starting transfers between devices, spread_weights(): lax.ppermute(pieces[k], 'group', [(0, 2 * k)])  19.7 us
    pallas_call x2, Pallas kernels, product(): pl.pallas_call(functools.partial(product_kernel, count, len(lines)), out_...  17.2 us
    ppermute x3, waiting for transfers between devices, spread_weights(): held.append(lax.ppermute(held[-1], ('group', 'tp'), ring_pairs((0, 1))))  10.9 us
    ppermute x6, starting transfers between devices, over_y(): lax.ppermute(parts[step], 'tp', tp_pairs(0, step, 0))  10.1 us
    ppermute x5, starting transfers between devices, to_core(): return lax.ppermute(value, 'tp', tp_pairs(0, 0, 1))  9.09 us
    ppermute x4, waiting for transfers between devices, over_x(): return lax.ppermute(value, 'tp', tp_pairs(1, 0, 0))  8.99 us
    unnamed x49, local copies, waits for them, and re-layouts  7.48 us
  transfers between devices with their start and end apart: 29, of which 12 were waited for; matrix products, arithmetic and copies ran while one was open for 3% of the time, Pallas kernels for 17%

profile of v2, /device:TPU:8, one launch (start us, length us, event | category | flops | bytes accessed | tf_op | source)
XLA Modules:
  0.0 187.2 jit_solution(896047750805382987)
XLA Ops:
  0.0 2.4 %shard_map.64 = bf16[10,2,4,16,512]{4,3,2,1,0:T(8,128)(2,1)} custom-call(bf16[16,2,4,16,512]{4,3,2,1,0:T(8,128)(2,1)} %bitcast.27), custom_call_target="tpu_custom_call" | custom-call | tf_op jit(solution)/shard_map/pallas_call | solution.py:348
  4.6 3.5 %shard_map.65 = (bf16[2,512,128]{2,1,0:T(8,128)(2,1)}, bf16[2,512,128]{2,1,0:T(8,128)(2,1)}, bf16[2,512,128]{2,1,0:T(8,128)(2,1)}, bf16[2,512,128]{2,1,0:T(8,128...) custom-call(bf16[1,512]{1,0:T(2,128)(2,1)} %broadcast_in_dim.6.gain_, ...), custom_call_target="tpu_custom_call" | custom-call | tf_op jit(solution)/shard_map/pallas_call | solution.py:95
  8.1 9.1 %collective-permute-start.2 = (bf16[2,512,128]{2,1,0:T(8,128)(2,1)}, bf16[2,512,128]{2,1,0:T(8,128)(2,1)S(1)}, u32[]{:S(2)}, u32[]{:S(2)}) collective-permute-start(bf16[2,512,128]{2,1,0:T(8,128)(2,1)} %get-tuple-element.27), channel_id=1, source_target_pairs={{0,128},{1,129},{2,130},{3,131},{4,132},{5,133},{6,134},{7,135},{8... | collective-permute-start | bytes 786440 | tf_op jit(solution)/shard_map/ppermute | solution.py:133
  19.8 4.3 %collective-permute-done.2.refs_1_ = bf16[2,512,128]{2,1,0:T(8,128)(2,1)S(1)} collective-permute-done((bf16[2,512,128]{2,1,0:T(8,128)(2,1)}, bf16[2,512,128]{2,1,0:T(8,128)(2,1)S(1)}, u32[]{:S(2)}, u32[]{:S(2)}) %collective-permute-start.2) | collective-permute-done | bytes 262176 | tf_op jit(solution)/shard_map/ppermute | solution.py:133
  24.1 2.0 %collective-permute-start.5 = (bf16[2,512,128]{2,1,0:T(8,128)(2,1)}, bf16[2,512,128]{2,1,0:T(8,128)(2,1)}, u32[]{:S(2)}, u32[]{:S(2)}) collective-permute-start(bf16[2,512,128]{2,1,0:T(8,128)(2,1)} %get-tuple-element.30), channel_id=1, source_target_pairs={{0,192},{1,193},{2,194},{3,195},{4,196},{5,197},{6,198},{7,199},{8... | collective-permute-start | bytes 786440 | tf_op jit(solution)/shard_map/ppermute | solution.py:133
  26.1 2.0 %collective-permute-start.6 = (bf16[2,512,128]{2,1,0:T(8,128)(2,1)}, bf16[2,512,128]{2,1,0:T(8,128)(2,1)}, u32[]{:S(2)}, u32[]{:S(2)}) collective-permute-start(bf16[2,512,128]{2,1,0:T(8,128)(2,1)} %get-tuple-element.31), channel_id=1, source_target_pairs={{0,64},{1,65},{2,66},{3,67},{4,68},{5,69},{6,70},{7,71},{8,72},{9,... | collective-permute-start | bytes 786440 | tf_op jit(solution)/shard_map/ppermute | solution.py:133
  29.8 2.0 %collective-permute-start.7 = (bf16[2,512,128]{2,1,0:T(8,128)(2,1)}, bf16[2,512,128]{2,1,0:T(8,128)(2,1)}, u32[]{:S(2)}, u32[]{:S(2)}) collective-permute-start(bf16[2,512,128]{2,1,0:T(8,128)(2,1)} %get-tuple-element.32), channel_id=1, source_target_pairs={{0,224},{1,225},{2,226},{3,227},{4,228},{5,229},{6,230},{7,231},{8... | collective-permute-start | bytes 786440 | tf_op jit(solution)/shard_map/ppermute | solution.py:133
  31.8 2.0 %collective-permute-start.8 = (bf16[2,512,128]{2,1,0:T(8,128)(2,1)}, bf16[2,512,128]{2,1,0:T(8,128)(2,1)}, u32[]{:S(2)}, u32[]{:S(2)}) collective-permute-start(bf16[2,512,128]{2,1,0:T(8,128)(2,1)} %get-tuple-element.33), channel_id=1, source_target_pairs={{0,32},{1,33},{2,34},{3,35},{4,36},{5,37},{6,38},{7,39},{8,40},{9,... | collective-permute-start | bytes 786440 | tf_op jit(solution)/shard_map/ppermute | solution.py:133
  33.8 2.0 %shard_map.66.refs_9_.refs_0_ = bf16[6,2,4,16,512]{4,3,2,1,0:T(8,128)(2,1)} custom-call(bf16[16,2,4,16,512]{4,3,2,1,0:T(8,128)(2,1)} %bitcast.28, bf16[2,512,128]{2,1,0:T(8,128)(2,1)} %get-tuple-element.26.refs_0_), custom_call_target="tpu_custom_call" | custom-call | tf_op jit(solution)/shard_map/pallas_call | solution.py:348
  36.4 4.4 %shard_map.67.refs_10_.refs_9_ = bf16[4,16,256]{2,1,0:T(8,128)(2,1)} custom-call(s32[4]{0:T(128)} %pad_add_fusion.where_ref, bf16[16,2,4,16,512]{4,3,2,1,0:T(8,128)(2,1)} %bitcast.29, bf16[16,2,4,16,512]{4,3,2,1,0:T(8,128)(2,1)} %copy-done), custom_call_target="tpu_custom_call" | custom-call | tf_op jit(solution)/shard_map/pallas_call | solution.py:330
  42.0 2.5 %shard_map.68 = bf16[2,512,128]{2,1,0:T(8,128)(2,1)} custom-call(s32[1]{0:T(128)} %bitcast.9.learner_ref, bf16[2,512,128]{2,1,0:T(8,128)(2,1)} %get-tuple-element.26.refs_0_, bf16[2,512,128]{2,1,0:T(8,128)(2,1)} %copy-done.11, bf16[2,512,128]{2,1,0:T(8,128)(2,1)} %copy-done.12, bf16[2,512,128]{2,1,0:T(8,128)(2,1)} %copy-done.13, ...), custom_call_target="tpu_custom_call" | custom-call | tf_op jit(solution)/shard_map/pallas_call | solution.py:121
  46.0 5.0 %collective-permute-done.9 = bf16[2,512,128]{2,1,0:T(8,128)(2,1)S(1)} collective-permute-done((bf16[2,512,128]{2,1,0:T(8,128)(2,1)}, bf16[2,512,128]{2,1,0:T(8,128)(2,1)S(1)}, u32[]{:S(2)}, u32[]{:S(2)}) %collective-permute-start.9) | collective-permute-done | bytes 262176 | tf_op jit(solution)/shard_map/ppermute | solution.py:136
  54.3 4.2 %collective-permute-done.10.refs_1_ = bf16[512,128]{1,0:T(8,128)(2,1)S(1)} collective-permute-done((bf16[512,128]{1,0:T(8,128)(2,1)S(1)}, bf16[512,128]{1,0:T(8,128)(2,1)S(1)}, u32[]{:S(2)}, u32[]{:S(2)}) %collective-permute-start.10) | collective-permute-done | bytes 131104 | tf_op jit(solution)/shard_map/ppermute | solution.py:301
  60.1 2.6 %collective-permute-start.16 = (bf16[2048,128]{1,0:T(8,128)(2,1)S(1)}, bf16[2048,128]{1,0:T(8,128)(2,1)}, u32[]{:S(2)}, u32[]{:S(2)}) collective-permute-start(bf16[2048,128]{1,0:T(8,128)(2,1)S(1)} %pad_maximum_fusion.refs_6_), channel_id=1, source_target_pairs={{0,32},{1,225},{2,34},{3,227},{4,36},{5,229},{6,38},{7,231},{8,40}... | collective-permute-start | bytes 1572872 | tf_op jit(solution)/shard_map/ppermute | solution.py:143
  62.7 2.3 %collective-permute-start.12 = (bf16[10,2,4,16,512]{4,3,2,1,0:T(8,128)(2,1)S(1)}, bf16[10,2,4,16,512]{4,3,2,1,0:T(8,128)(2,1)S(1)}, u32[]{:S(2)}, u32[]{:S(2)}) collective-permute-start(bf16[10,2,4,16,512]{4,3,2,1,0:T(8,128)(2,1)S(1)} %copy-done.2), channel_id=1, source_target_pairs={{0,1},{1,0},{2,3},{3,2},{4,5},{5,4},{6,7},{7,6},{8,9},{9,8},{10,11... | collective-permute-start | bytes 3932168 | tf_op jit(solution)/shard_map/ppermute | solution.py:50
  65.0 5.7 %collective-permute-done.16.refs_7_ = bf16[2048,128]{1,0:T(8,128)(2,1)} collective-permute-done((bf16[2048,128]{1,0:T(8,128)(2,1)S(1)}, bf16[2048,128]{1,0:T(8,128)(2,1)}, u32[]{:S(2)}, u32[]{:S(2)}) %collective-permute-start.16) | collective-permute-done | bytes 524320 | tf_op jit(solution)/shard_map/ppermute | solution.py:143
  72.0 4.8 %collective-permute-done.11.refs_3_ = bf16[6,2,4,16,512]{4,3,2,1,0:T(8,128)(2,1)S(1)} collective-permute-done((bf16[6,2,4,16,512]{4,3,2,1,0:T(8,128)(2,1)}, bf16[6,2,4,16,512]{4,3,2,1,0:T(8,128)(2,1)S(1)}, u32[]{:S(2)}, u32[]{:S(2)}) %collective-permute-start.11) | collective-permute-done | bytes 786464 | tf_op jit(solution)/shard_map/ppermute | solution.py:301
  77.1 4.3 %collective-permute-done.17.refs_8_.refs_6_ = bf16[2048,128]{1,0:T(8,128)(2,1)} collective-permute-done((bf16[2048,128]{1,0:T(8,128)(2,1)}, bf16[2048,128]{1,0:T(8,128)(2,1)}, u32[]{:S(2)}, u32[]{:S(2)}) %collective-permute-start.17) | collective-permute-done | bytes 524320 | tf_op jit(solution)/shard_map/ppermute | solution.py:143
  82.6 8.6 %shard_map.70 = (bf16[528,256]{1,0:T(8,128)(2,1)}, bf16[528,256]{1,0:T(8,128)(2,1)}, bf16[528,256]{1,0:T(8,128)(2,1)}, bf16[528,256]{1,0:T(8,128)(2,1)}) custom-call(s32[4]{0:T(128)} %pad_add_fusion.where_ref, bf16[16,2,4,16,512]{4,3,2,1,0:T(8,128)(2,1)} %bitcast.30, bf16[16,2,4,16,512]{4,3,2,1,0:T(8,128)(2,1)} %copy-done, ...), custom_call_target="tpu_custom_call" | custom-call | flops 2147483648 | bytes 10485760 | tf_op jit(solution)/shard_map/pallas_call | solution.py:188
  95.9 2.4 %collective-permute-start.20 = (bf16[528,256]{1,0:T(8,128)(2,1)}, bf16[528,256]{1,0:T(8,128)(2,1)S(1)}, u32[]{:S(2)}, u32[]{:S(2)}) collective-permute-start(bf16[528,256]{1,0:T(8,128)(2,1)} %get-tuple-element.37), channel_id=1, source_target_pairs={{0,6},{1,7},{2,0},{3,1},{4,2},{5,3},{6,4},{7,5},{8,14},{9,15},{10,... | collective-permute-start | bytes 811016 | tf_op jit(solution)/shard_map/ppermute | solution.py:296
  98.3 2.0 %collective-permute-done.18.refs_1_.refs_9_ = bf16[528,256]{1,0:T(8,128)(2,1)S(1)} collective-permute-done((bf16[528,256]{1,0:T(8,128)(2,1)}, bf16[528,256]{1,0:T(8,128)(2,1)S(1)}, u32[]{:S(2)}, u32[]{:S(2)}) %collective-permute-start.18) | collective-permute-done | bytes 270368 | tf_op jit(solution)/shard_map/ppermute | solution.py:296
  101.8 8.5 %shard_map.73 = (bf16[512,256]{1,0:T(8,128)(2,1)}, bf16[512,256]{1,0:T(8,128)(2,1)}, bf16[512,256]{1,0:T(8,128)(2,1)}, bf16[512,256]{1,0:T(8,128)(2,1)}) custom-call(s32[4]{0:T(128)} %pad_add_fusion.where_ref, bf16[16,2,4,16,512]{4,3,2,1,0:T(8,128)(2,1)} %bitcast.31, bf16[16,2,4,16,512]{4,3,2,1,0:T(8,128)(2,1)} %copy-done, ...), custom_call_target="tpu_custom_call" | custom-call | flops 2147483648 | bytes 10485760 | tf_op jit(solution)/shard_map/pallas_call | solution.py:188
  110.4 1.8 collective-permute-start.23
  112.2 2.0 %collective-permute-start.24 = (bf16[512,256]{1,0:T(8,128)(2,1)}, bf16[512,256]{1,0:T(8,128)(2,1)S(1)}, u32[]{:S(2)}, u32[]{:S(2)}) collective-permute-start(bf16[512,256]{1,0:T(8,128)(2,1)} %get-tuple-element.40), channel_id=1, source_target_pairs={{0,4},{1,5},{2,6},{3,7},{4,0},{5,1},{6,2},{7,3},{8,12},{9,13},{10,... | collective-permute-start | bytes 786440 | tf_op jit(solution)/shard_map/ppermute | solution.py:296
  116.4 2.2 %shard_map.71.summed_ref = f32[528,256]{1,0:T(8,128)} custom-call(bf16[528,256]{1,0:T(8,128)(2,1)} %get-tuple-element.34.refs_0_, bf16[528,256]{1,0:T(8,128)(2,1)} %copy-done.6, bf16[528,256]{1,0:T(8,128)(2,1)} %copy-done.9, bf16[528,256]{1,0:T(8,128)(2,1)} %copy-done.10), custom_call_target="tpu_custom_call" | custom-call | tf_op jit(solution)/shard_map/pallas_call | solution.py:220
  120.4 3.1 %collective-permute-done.25.refs_3_ = bf16[512,256]{1,0:T(8,128)(2,1)S(1)} collective-permute-done((bf16[512,256]{1,0:T(8,128)(2,1)}, bf16[512,256]{1,0:T(8,128)(2,1)S(1)}, u32[]{:S(2)}, u32[]{:S(2)}) %collective-permute-start.25) | collective-permute-done | bytes 262176 | tf_op jit(solution)/shard_map/ppermute | solution.py:296
  124.2 3.2 %shard_map.74 = (bf16[128,512]{1,0:T(8,128)(2,1)}, bf16[128,512]{1,0:T(8,128)(2,1)}, bf16[144,512]{1,0:T(8,128)(2,1)}, bf16[128,512]{1,0:T(8,128)(2,1)}, f32[2,256]{1,0:T(2,128)}) custom-call(s32[4]{0:T(128)} %pad_add_fusion.where_ref, f32[528,256]{1,0:T(8,128)} %shard_map.71.summed_ref, bf16[512,256]{1,0:T(8,128)(2,1)} %get-tuple-element.38.refs_0_, ...), custom_call_target="tpu_custom_call" | custom-call | tf_op jit(solution)/shard_map/pallas_call | solution.py:263
  127.3 5.2 %collective-permute-start.26 = (bf16[128,512]{1,0:T(8,128)(2,1)}, bf16[128,512]{1,0:T(8,128)(2,1)S(1)}, u32[]{:S(2)}, u32[]{:S(2)}) collective-permute-start(bf16[128,512]{1,0:T(8,128)(2,1)} %get-tuple-element.44), channel_id=1, source_target_pairs={{0,1},{1,0},{2,3},{3,2},{4,5},{5,4},{6,7},{7,6},{8,9},{9,8},{10,11... | collective-permute-start | bytes 393224 | tf_op jit(solution)/shard_map/ppermute | solution.py:50
  132.5 2.9 %collective-permute-start.27 = (bf16[144,512]{1,0:T(8,128)(2,1)}, bf16[144,512]{1,0:T(8,128)(2,1)S(1)}, u32[]{:S(2)}, u32[]{:S(2)}) collective-permute-start(bf16[144,512]{1,0:T(8,128)(2,1)} %get-tuple-element.45), channel_id=1, source_target_pairs={{0,8},{1,9},{2,10},{3,11},{4,12},{5,13},{6,14},{7,15},{8,0},{9,1},... | collective-permute-start | bytes 442376 | tf_op jit(solution)/shard_map/ppermute | solution.py:301
  138.8 3.8 %collective-permute-done.28.refs_3_ = bf16[128,512]{1,0:T(8,128)(2,1)S(1)} collective-permute-done((bf16[128,512]{1,0:T(8,128)(2,1)}, bf16[128,512]{1,0:T(8,128)(2,1)S(1)}, u32[]{:S(2)}, u32[]{:S(2)}) %collective-permute-start.28) | collective-permute-done | bytes 131104 | tf_op jit(solution)/shard_map/ppermute | solution.py:452
  143.3 3.7 %shard_map.75 = bf16[16,16,2048]{2,1,0:T(8,128)(2,1)} custom-call(s32[4]{0:T(128)} %pad_add_fusion.where_ref, s32[32]{0:T(128)} %select_reduce_fusion.source_ref, s32[32]{0:T(128)} %convert_element_type.24.filled_ref, f32[2,256]{1,0:T(2,128)} %get-tuple-element.42.lines_ref, f32[128,1]{1,0:T(8,128)} %reshape.76.live_ref, f32[2,128,128]{2,1,0:T(8,128)} %stack.33.cos_ref, ...), custom_call_target="tpu_custom_call" | custom-call | tf_op jit(solution)/shard_map/pallas_call | solution.py:399
  147.0 39.3 %all_to_all.5 = bf16[16,16,2048]{2,1,0:T(8,128)(2,1)S(1)} all-to-all(bf16[16,16,2048]{2,1,0:T(8,128)(2,1)} %shard_map.75), channel_id=1, replica_groups=mesh['group'=16,'tp'=16] {'group'}, dimensions={0} | all-to-all | bytes 2097152 | tf_op jit(solution)/shard_map/all_to_all | solution.py:468
  (111 shorter events, 33.1 us)
Async XLA Ops:
  0.0 31.8 %collective-permute-start = (bf16[16,2,4,16,512]{4,3,2,1,0:T(8,128)(2,1)}, bf16[16,2,4,16,512]{4,3,2,1,0:T(8,128)(2,1)S(1)}, u32[]{:S(2)}, u32[]{:S(2)}) collective-permute-start(bf16[16,2,4,16,512]{4,3,2,1,0:T(8,128)(2,1)} %bitcast.26), channel_id=1, source_target_pairs={{0,1},{1,0},{2,3},{3,2},{4,5},{5,4},{6,7},{7,6},{8,9},{9,8},{10,11... | collective-permute-start | bytes 6291464 | tf_op jit(solution)/shard_map/ppermute | solution.py:50
  2.4 38.5 %collective-permute-start.1 = (bf16[10,2,4,16,512]{4,3,2,1,0:T(8,128)(2,1)}, bf16[10,2,4,16,512]{4,3,2,1,0:T(8,128)(2,1)S(1)}, u32[]{:S(2)}, u32[]{:S(2)}) collective-permute-start(bf16[10,2,4,16,512]{4,3,2,1,0:T(8,128)(2,1)} %shard_map.64), channel_id=1, source_target_pairs={{0,8},{1,9},{2,10},{3,11},{4,12},{5,13},{6,14},{7,15},{8,0},{9,1},... | collective-permute-start | bytes 3932168 | tf_op jit(solution)/shard_map/ppermute | solution.py:301
  8.1 16.0 %collective-permute-start.2 = (bf16[2,512,128]{2,1,0:T(8,128)(2,1)}, bf16[2,512,128]{2,1,0:T(8,128)(2,1)S(1)}, u32[]{:S(2)}, u32[]{:S(2)}) collective-permute-start(bf16[2,512,128]{2,1,0:T(8,128)(2,1)} %get-tuple-element.27), channel_id=1, source_target_pairs={{0,128},{1,129},{2,130},{3,131},{4,132},{5,133},{6,134},{7,135},{8... | collective-permute-start | bytes 786440 | tf_op jit(solution)/shard_map/ppermute | solution.py:133
  17.2 8.9 %collective-permute-start.3 = (bf16[2,512,128]{2,1,0:T(8,128)(2,1)}, bf16[2,512,128]{2,1,0:T(8,128)(2,1)S(1)}, u32[]{:S(2)}, u32[]{:S(2)}) collective-permute-start(bf16[2,512,128]{2,1,0:T(8,128)(2,1)} %get-tuple-element.28), channel_id=1, source_target_pairs={{0,160},{1,161},{2,162},{3,163},{4,164},{5,165},{6,166},{7,167},{8... | collective-permute-start | bytes 786440 | tf_op jit(solution)/shard_map/ppermute | solution.py:133
  18.5 11.2 %collective-permute-start.4 = (bf16[2,512,128]{2,1,0:T(8,128)(2,1)}, bf16[2,512,128]{2,1,0:T(8,128)(2,1)S(1)}, u32[]{:S(2)}, u32[]{:S(2)}) collective-permute-start(bf16[2,512,128]{2,1,0:T(8,128)(2,1)} %get-tuple-element.29), channel_id=1, source_target_pairs={{0,96},{1,97},{2,98},{3,99},{4,100},{5,101},{6,102},{7,103},{8,104... | collective-permute-start | bytes 786440 | tf_op jit(solution)/shard_map/ppermute | solution.py:133
  24.1 16.7 %collective-permute-start.5 = (bf16[2,512,128]{2,1,0:T(8,128)(2,1)}, bf16[2,512,128]{2,1,0:T(8,128)(2,1)}, u32[]{:S(2)}, u32[]{:S(2)}) collective-permute-start(bf16[2,512,128]{2,1,0:T(8,128)(2,1)} %get-tuple-element.30), channel_id=1, source_target_pairs={{0,192},{1,193},{2,194},{3,195},{4,196},{5,197},{6,198},{7,199},{8... | collective-permute-start | bytes 786440 | tf_op jit(solution)/shard_map/ppermute | solution.py:133
  26.1 14.7 %collective-permute-start.6 = (bf16[2,512,128]{2,1,0:T(8,128)(2,1)}, bf16[2,512,128]{2,1,0:T(8,128)(2,1)}, u32[]{:S(2)}, u32[]{:S(2)}) collective-permute-start(bf16[2,512,128]{2,1,0:T(8,128)(2,1)} %get-tuple-element.31), channel_id=1, source_target_pairs={{0,64},{1,65},{2,66},{3,67},{4,68},{5,69},{6,70},{7,71},{8,72},{9,... | collective-permute-start | bytes 786440 | tf_op jit(solution)/shard_map/ppermute | solution.py:133
  29.8 11.1 %collective-permute-start.7 = (bf16[2,512,128]{2,1,0:T(8,128)(2,1)}, bf16[2,512,128]{2,1,0:T(8,128)(2,1)}, u32[]{:S(2)}, u32[]{:S(2)}) collective-permute-start(bf16[2,512,128]{2,1,0:T(8,128)(2,1)} %get-tuple-element.32), channel_id=1, source_target_pairs={{0,224},{1,225},{2,226},{3,227},{4,228},{5,229},{6,230},{7,231},{8... | collective-permute-start | bytes 786440 | tf_op jit(solution)/shard_map/ppermute | solution.py:133
  31.8 9.1 %collective-permute-start.8 = (bf16[2,512,128]{2,1,0:T(8,128)(2,1)}, bf16[2,512,128]{2,1,0:T(8,128)(2,1)}, u32[]{:S(2)}, u32[]{:S(2)}) collective-permute-start(bf16[2,512,128]{2,1,0:T(8,128)(2,1)} %get-tuple-element.33), channel_id=1, source_target_pairs={{0,32},{1,33},{2,34},{3,35},{4,36},{5,37},{6,38},{7,39},{8,40},{9,... | collective-permute-start | bytes 786440 | tf_op jit(solution)/shard_map/ppermute | solution.py:133
  44.5 32.3 %copy-start.20 = (s32[1,16]{1,0:T(1,128)S(1)}, s32[1,16]{1,0:T(1,128)}, u32[]{:S(2)}) copy-start(s32[1,16]{1,0:T(1,128)} %param.9) | copy-start | bytes 196
  44.5 32.6 %copy-start.23 = (s32[1,16]{1,0:T(1,128)S(1)}, s32[1,16]{1,0:T(1,128)}, u32[]{:S(2)}) copy-start(s32[1,16]{1,0:T(1,128)} %param.11) | copy-start | bytes 196
  44.5 6.5 %collective-permute-start.9 = (bf16[2,512,128]{2,1,0:T(8,128)(2,1)}, bf16[2,512,128]{2,1,0:T(8,128)(2,1)S(1)}, u32[]{:S(2)}, u32[]{:S(2)}) collective-permute-start(bf16[2,512,128]{2,1,0:T(8,128)(2,1)} %shard_map.68), channel_id=1, source_target_pairs={{0,16},{32,48},{64,80},{96,112},{128,144},{160,176},{192,208},{224... | collective-permute-start | bytes 786440 | tf_op jit(solution)/shard_map/ppermute | solution.py:136
  52.1 6.5 %collective-permute-start.10 = (bf16[512,128]{1,0:T(8,128)(2,1)S(1)}, bf16[512,128]{1,0:T(8,128)(2,1)S(1)}, u32[]{:S(2)}, u32[]{:S(2)}) collective-permute-start(bf16[512,128]{1,0:T(8,128)(2,1)S(1)} %get-tuple-element.48), channel_id=1, source_target_pairs={{0,8},{1,9},{2,10},{3,11},{4,12},{5,13},{6,14},{7,15},{8,0},{9,1},... | collective-permute-start | bytes 393224 | tf_op jit(solution)/shard_map/ppermute | solution.py:301
  52.7 6.5 %collective-permute-start.15 = (bf16[512,128]{1,0:T(8,128)(2,1)S(1)}, bf16[512,128]{1,0:T(8,128)(2,1)S(1)}, u32[]{:S(2)}, u32[]{:S(2)}) collective-permute-start(bf16[512,128]{1,0:T(8,128)(2,1)S(1)} %get-tuple-element.48), channel_id=1, source_target_pairs={{0,9},{1,8},{2,11},{3,10},{4,13},{5,12},{6,15},{7,14},{8,1},{9,0},... | collective-permute-start | bytes 393224 | tf_op jit(solution)/shard_map/ppermute | solution.py:140
  52.7 6.5 %collective-permute-start.14 = (bf16[512,128]{1,0:T(8,128)(2,1)S(1)}, bf16[512,128]{1,0:T(8,128)(2,1)S(1)}, u32[]{:S(2)}, u32[]{:S(2)}) collective-permute-start(bf16[512,128]{1,0:T(8,128)(2,1)S(1)} %get-tuple-element.47), channel_id=1, source_target_pairs={{0,1},{1,0},{2,3},{3,2},{4,5},{5,4},{6,7},{7,6},{8,9},{9,8},{10,11... | collective-permute-start | bytes 393224 | tf_op jit(solution)/shard_map/ppermute | solution.py:50
  59.2 17.6 %collective-permute-start.11 = (bf16[6,2,4,16,512]{4,3,2,1,0:T(8,128)(2,1)}, bf16[6,2,4,16,512]{4,3,2,1,0:T(8,128)(2,1)S(1)}, u32[]{:S(2)}, u32[]{:S(2)}) collective-permute-start(bf16[6,2,4,16,512]{4,3,2,1,0:T(8,128)(2,1)} %shard_map.69), channel_id=1, source_target_pairs={{0,8},{1,9},{2,10},{3,11},{4,12},{5,13},{6,14},{7,15},{8,0},{9,1},... | collective-permute-start | bytes 2359304 | tf_op jit(solution)/shard_map/ppermute | solution.py:301
  60.1 10.6 %collective-permute-start.16 = (bf16[2048,128]{1,0:T(8,128)(2,1)S(1)}, bf16[2048,128]{1,0:T(8,128)(2,1)}, u32[]{:S(2)}, u32[]{:S(2)}) collective-permute-start(bf16[2048,128]{1,0:T(8,128)(2,1)S(1)} %pad_maximum_fusion.refs_6_), channel_id=1, source_target_pairs={{0,32},{1,225},{2,34},{3,227},{4,36},{5,229},{6,38},{7,231},{8,40}... | collective-permute-start | bytes 1572872 | tf_op jit(solution)/shard_map/ppermute | solution.py:143
  62.7 18.9 %collective-permute-start.12 = (bf16[10,2,4,16,512]{4,3,2,1,0:T(8,128)(2,1)S(1)}, bf16[10,2,4,16,512]{4,3,2,1,0:T(8,128)(2,1)S(1)}, u32[]{:S(2)}, u32[]{:S(2)}) collective-permute-start(bf16[10,2,4,16,512]{4,3,2,1,0:T(8,128)(2,1)S(1)} %copy-done.2), channel_id=1, source_target_pairs={{0,1},{1,0},{2,3},{3,2},{4,5},{5,4},{6,7},{7,6},{8,9},{9,8},{10,11... | collective-permute-start | bytes 3932168 | tf_op jit(solution)/shard_map/ppermute | solution.py:50
  70.7 10.7 %collective-permute-start.17 = (bf16[2048,128]{1,0:T(8,128)(2,1)}, bf16[2048,128]{1,0:T(8,128)(2,1)}, u32[]{:S(2)}, u32[]{:S(2)}) collective-permute-start(bf16[2048,128]{1,0:T(8,128)(2,1)} %collective-permute-done.16.refs_7_), channel_id=1, source_target_pairs={{0,32},{1,225},{2,34},{3,227},{4,36},{5,229},{6,38},{7,231},{8,40}... | collective-permute-start | bytes 1572872 | tf_op jit(solution)/shard_map/ppermute | solution.py:143
  76.7 4.8 %collective-permute-start.13 = (bf16[6,2,4,16,512]{4,3,2,1,0:T(8,128)(2,1)S(1)}, bf16[6,2,4,16,512]{4,3,2,1,0:T(8,128)(2,1)}, u32[]{:S(2)}, u32[]{:S(2)}) collective-permute-start(bf16[6,2,4,16,512]{4,3,2,1,0:T(8,128)(2,1)S(1)} %collective-permute-done.11.refs_3_), channel_id=1, source_target_pairs={{0,1},{1,0},{2,3},{3,2},{4,5},{5,4},{6,7},{7,6},{8,9},{9,8},{10,11... | collective-permute-start | bytes 2359304 | tf_op jit(solution)/shard_map/ppermute | solution.py:50
  81.4 10.7 %collective-permute-start.21 = (bf16[2048,128]{1,0:T(8,128)(2,1)}, bf16[2048,128]{1,0:T(8,128)(2,1)}, u32[]{:S(2)}, u32[]{:S(2)}) collective-permute-start(bf16[2048,128]{1,0:T(8,128)(2,1)} %collective-permute-done.17.refs_8_.refs_6_), channel_id=1, source_target_pairs={{0,32},{1,225},{2,34},{3,227},{4,36},{5,229},{6,38},{7,231},{8,40}... | collective-permute-start | bytes 1572872 | tf_op jit(solution)/shard_map/ppermute | solution.py:143
  92.1 8.2 %collective-permute-start.22 = (bf16[2048,128]{1,0:T(8,128)(2,1)}, bf16[2048,128]{1,0:T(8,128)(2,1)S(1)}, u32[]{:S(2)}, u32[]{:S(2)}) collective-permute-start(bf16[2048,128]{1,0:T(8,128)(2,1)} %shard_map.72.refs_7_), channel_id=1, source_target_pairs={{1,225},{3,227},{5,229},{7,231},{9,233},{11,235},{13,237},{15,239}... | collective-permute-start | bytes 1572872 | tf_op jit(solution)/shard_map/ppermute | solution.py:447
  92.8 7.5 %collective-permute-start.18 = (bf16[528,256]{1,0:T(8,128)(2,1)}, bf16[528,256]{1,0:T(8,128)(2,1)S(1)}, u32[]{:S(2)}, u32[]{:S(2)}) collective-permute-start(bf16[528,256]{1,0:T(8,128)(2,1)} %get-tuple-element.35.refs_1_), channel_id=1, source_target_pairs={{0,2},{1,3},{2,4},{3,5},{4,6},{5,7},{6,0},{7,1},{8,10},{9,11},{10,... | collective-permute-start | bytes 811016 | tf_op jit(solution)/shard_map/ppermute | solution.py:296
  94.9 20.7 %collective-permute-start.19 = (bf16[528,256]{1,0:T(8,128)(2,1)}, bf16[528,256]{1,0:T(8,128)(2,1)S(1)}, u32[]{:S(2)}, u32[]{:S(2)}) collective-permute-start(bf16[528,256]{1,0:T(8,128)(2,1)} %get-tuple-element.36), channel_id=1, source_target_pairs={{0,4},{1,5},{2,6},{3,7},{4,0},{5,1},{6,2},{7,3},{8,12},{9,13},{10,... | collective-permute-start | bytes 811016 | tf_op jit(solution)/shard_map/ppermute | solution.py:296
  95.9 19.6 %copy-start.22 = (s32[1,16]{1,0:T(1,128)S(1)}, s32[1,16]{1,0:T(1,128)}, u32[]{:S(2)}) copy-start(s32[1,16]{1,0:T(1,128)} %param.10) | copy-start | bytes 196
  95.9 19.7 %collective-permute-start.20 = (bf16[528,256]{1,0:T(8,128)(2,1)}, bf16[528,256]{1,0:T(8,128)(2,1)S(1)}, u32[]{:S(2)}, u32[]{:S(2)}) collective-permute-start(bf16[528,256]{1,0:T(8,128)(2,1)} %get-tuple-element.37), channel_id=1, source_target_pairs={{0,6},{1,7},{2,0},{3,1},{4,2},{5,3},{6,4},{7,5},{8,14},{9,15},{10,... | collective-permute-start | bytes 811016 | tf_op jit(solution)/shard_map/ppermute | solution.py:296
  110.4 8.2 %collective-permute-start.23 = (bf16[512,256]{1,0:T(8,128)(2,1)}, bf16[512,256]{1,0:T(8,128)(2,1)S(1)}, u32[]{:S(2)}, u32[]{:S(2)}) collective-permute-start(bf16[512,256]{1,0:T(8,128)(2,1)} %get-tuple-element.39), channel_id=1, source_target_pairs={{0,2},{1,3},{2,4},{3,5},{4,6},{5,7},{6,0},{7,1},{8,10},{9,11},{10,... | collective-permute-start | bytes 786440 | tf_op jit(solution)/shard_map/ppermute | solution.py:296
  112.2 8.2 %collective-permute-start.24 = (bf16[512,256]{1,0:T(8,128)(2,1)}, bf16[512,256]{1,0:T(8,128)(2,1)S(1)}, u32[]{:S(2)}, u32[]{:S(2)}) collective-permute-start(bf16[512,256]{1,0:T(8,128)(2,1)} %get-tuple-element.40), channel_id=1, source_target_pairs={{0,4},{1,5},{2,6},{3,7},{4,0},{5,1},{6,2},{7,3},{8,12},{9,13},{10,... | collective-permute-start | bytes 786440 | tf_op jit(solution)/shard_map/ppermute | solution.py:296
  114.1 9.3 %collective-permute-start.25 = (bf16[512,256]{1,0:T(8,128)(2,1)}, bf16[512,256]{1,0:T(8,128)(2,1)S(1)}, u32[]{:S(2)}, u32[]{:S(2)}) collective-permute-start(bf16[512,256]{1,0:T(8,128)(2,1)} %get-tuple-element.41), channel_id=1, source_target_pairs={{0,6},{1,7},{2,0},{3,1},{4,2},{5,3},{6,4},{7,5},{8,14},{9,15},{10,... | collective-permute-start | bytes 786440 | tf_op jit(solution)/shard_map/ppermute | solution.py:296
  127.3 11.4 %collective-permute-start.26 = (bf16[128,512]{1,0:T(8,128)(2,1)}, bf16[128,512]{1,0:T(8,128)(2,1)S(1)}, u32[]{:S(2)}, u32[]{:S(2)}) collective-permute-start(bf16[128,512]{1,0:T(8,128)(2,1)} %get-tuple-element.44), channel_id=1, source_target_pairs={{0,1},{1,0},{2,3},{3,2},{4,5},{5,4},{6,7},{7,6},{8,9},{9,8},{10,11... | collective-permute-start | bytes 393224 | tf_op jit(solution)/shard_map/ppermute | solution.py:50
  132.5 10.1 %collective-permute-start.27 = (bf16[144,512]{1,0:T(8,128)(2,1)}, bf16[144,512]{1,0:T(8,128)(2,1)S(1)}, u32[]{:S(2)}, u32[]{:S(2)}) collective-permute-start(bf16[144,512]{1,0:T(8,128)(2,1)} %get-tuple-element.45), channel_id=1, source_target_pairs={{0,8},{1,9},{2,10},{3,11},{4,12},{5,13},{6,14},{7,15},{8,0},{9,1},... | collective-permute-start | bytes 442376 | tf_op jit(solution)/shard_map/ppermute | solution.py:301
  135.4 7.2 %collective-permute-start.28 = (bf16[128,512]{1,0:T(8,128)(2,1)}, bf16[128,512]{1,0:T(8,128)(2,1)S(1)}, u32[]{:S(2)}, u32[]{:S(2)}) collective-permute-start(bf16[128,512]{1,0:T(8,128)(2,1)} %get-tuple-element.46), channel_id=1, source_target_pairs={{0,9},{1,8},{2,11},{3,10},{4,13},{5,12},{6,15},{7,14},{8,1},{9,0},... | collective-permute-start | bytes 393224 | tf_op jit(solution)/shard_map/ppermute | solution.py:452
  (21 other events, 85.2 us)
